TPU v7x, 32 devices: a whole 2x2x4 slice. The times are simulated.
32 devices in a mesh: frames: 8 (over z, x), cols: 4 (over y, core).
Axes of the slice: x: 2, y: 2, z: 4, core: 2. Of those that a mesh axis runs over, the one named last changes fastest.
Arguments:
- right_side: float32 [6, 8192], P(None, ('frames', 'cols')), may hold values from -6 to 6
- diag_blocks: float32 [6, 6, 8192], P(None, None, ('frames', 'cols')), may hold values from -0.6 to 24, as said below
- band_blocks: float32 [8, 6, 6, 8192], P(None, None, None, ('frames', 'cols')), may hold values from -0.6 to 0.6
- reach: int32 [8192], P(('frames', 'cols')), may hold values from 1 to 8
- tiles: float32 [8, 4, 8, 384, 384], P('frames', 'cols'), may hold values from -0.09185587 to 0.09185587
- tile_rows: int32 [8, 4, 8], P('frames', 'cols'), may hold values from 0 to 15
- tile_cols: int32 [8, 4, 8], P('frames', 'cols'), may hold values from 0 to 31
- tile_count: int32 [8, 4], P('frames', 'cols'), may hold values from 1 to 8
Outputs:
- solution: float32 [6, 8192], P(None, ('frames', 'cols'))
- residual: float32 [6, 8192], P(None, ('frames', 'cols'))
Inputs may be any that keep to these rules, and one draw needn't show every extreme that they name: `diag_blocks`: each block is symmetric, with diagonal entries at least 6 and larger than the sum of its other entries' magnitudes in that row, so each block is positive definite.
All inputs are finite; a program needn't handle non-finite values.
Results may differ from a plain program's by a relative error of at most 0.0003.
Values sent between devices are 32-bit elements; how exact they have to be, the bound alone decides.
A program may use at most 64 MiB of HBM per device.

v0:
```python
import jax
import jax.numpy as jnp
from jax import lax
from jax.sharding import PartitionSpec as P

ITERS = 4


def shifted(value, axis, steps):
    count = lax.axis_size(axis)
    initial, last = (max(0, -steps), min(count, count - steps))
    return lax.ppermute(value, axis, [(source, source + steps) for source in range(initial, last)])


def invert_blocks(blocks):
    matrix_rows = [blocks[row_id] for row_id in range(6)]
    inverse = [jnp.zeros_like(blocks[0]).at[row_id].set(1.0) for row_id in range(6)]
    for pivot_id in range(6):
        pivot_value = matrix_rows[pivot_id][pivot_id]
        matrix_rows[pivot_id] = matrix_rows[pivot_id] / pivot_value
        inverse[pivot_id] = inverse[pivot_id] / pivot_value
        for row_id in range(6):
            if row_id != pivot_id:
                factor = matrix_rows[row_id][pivot_id]
                matrix_rows[row_id] = matrix_rows[row_id] - factor * matrix_rows[pivot_id]
                inverse[row_id] = inverse[row_id] - factor * inverse[pivot_id]
    return jnp.stack(inverse)


def precondition(inverse, vector):
    return jnp.einsum("abk,bk->ak", inverse, vector, precision=lax.Precision.HIGHEST)


def band_by_sums(vector, masked):
    band_len = masked.shape[0]
    frame_count = vector.shape[1]
    upper_rim = shifted(vector[:, :band_len], ("frames", "cols"), -1)
    extended = jnp.concatenate([vector, upper_rim], axis=1)
    result = jnp.zeros_like(vector)
    spill_over = jnp.zeros((6, frame_count + band_len), jnp.float32)
    for offset in range(1, band_len + 1):
        blocks_now = masked[offset - 1]
        result = result + jnp.einsum(
            "abk,bk->ak",
            blocks_now,
            extended[:, offset : offset + frame_count],
            precision=lax.Precision.HIGHEST,
        )
        back_term = jnp.einsum("abk,ak->bk", blocks_now, vector, precision=lax.Precision.HIGHEST)
        spill_over = spill_over.at[:, offset : offset + frame_count].add(back_term)
    carried = shifted(spill_over[:, frame_count:], ("frames", "cols"), 1)
    return (
        result
        + spill_over[:, :frame_count]
        + jnp.pad(carried, ((0, 0), (0, frame_count - band_len)))
    )


def loop_apply(vector, local_tiles, row_ids, col_ids, live_count):
    slot_total = local_tiles.shape[0]
    tile_side = local_tiles.shape[-1] // 6
    row_group = lax.all_gather(vector, "cols", axis=1, tiled=True)
    col_group = lax.all_gather(vector, "frames", axis=1, tiled=True)
    row_tiles = row_group.shape[1] // tile_side
    col_tiles = col_group.shape[1] // tile_side
    live_flag = (jnp.arange(slot_total, dtype=jnp.int32) < live_count).astype(jnp.float32)
    row_pick = (row_ids[:, None] == jnp.arange(row_tiles, dtype=jnp.int32)[None, :]).astype(
        jnp.float32
    )
    col_pick = (col_ids[:, None] == jnp.arange(col_tiles, dtype=jnp.int32)[None, :]).astype(
        jnp.float32
    )
    row_pieces = jnp.einsum(
        "sr,art->sat",
        row_pick,
        row_group.reshape(6, row_tiles, tile_side),
        precision=lax.Precision.HIGHEST,
    ).reshape(slot_total, 6 * tile_side)
    col_pieces = jnp.einsum(
        "sc,act->sat",
        col_pick,
        col_group.reshape(6, col_tiles, tile_side),
        precision=lax.Precision.HIGHEST,
    ).reshape(slot_total, 6 * tile_side)
    gain_row = (
        jnp.einsum("skn,sn->sk", local_tiles, col_pieces, precision=lax.Precision.HIGHEST)
        * live_flag[:, None]
    )
    gain_col = (
        jnp.einsum("sk,skn->sn", row_pieces, local_tiles, precision=lax.Precision.HIGHEST)
        * live_flag[:, None]
    )
    row_acc = jnp.einsum(
        "sr,sat->art",
        row_pick,
        gain_row.reshape(slot_total, 6, tile_side),
        precision=lax.Precision.HIGHEST,
    ).reshape(6, row_tiles * tile_side)
    col_acc = jnp.einsum(
        "sc,sat->act",
        col_pick,
        gain_col.reshape(slot_total, 6, tile_side),
        precision=lax.Precision.HIGHEST,
    ).reshape(6, col_tiles * tile_side)
    mine_rows = lax.psum_scatter(row_acc, "cols", scatter_dimension=1, tiled=True)
    mine_cols = lax.psum_scatter(col_acc, "frames", scatter_dimension=1, tiled=True)
    return mine_rows + mine_cols


def total_pair(first, second):
    return lax.psum((first, second), ("frames", "cols"))


def per_device(
    right_side, diag_blocks, band_blocks, reach, tiles, tile_rows, tile_cols, tile_count
):
    band_len = band_blocks.shape[0]
    offsets = jnp.arange(1, band_len + 1, dtype=jnp.int32)
    keep_mask = (offsets[:, None] <= reach[None, :]).astype(jnp.float32)
    masked = band_blocks * keep_mask[:, None, None, :]
    inverse = invert_blocks(diag_blocks)
    local_tiles = tiles[0, 0]
    row_ids = tile_rows[0, 0]
    col_ids = tile_cols[0, 0]
    live_count = tile_count[0, 0]
    solution = jnp.zeros_like(right_side)
    residual = right_side
    direction = residual
    along = residual
    gamma_old = jnp.float32(1.0)
    alpha_old = jnp.float32(1.0)
    for iteration in range(ITERS):
        precond = precondition(inverse, residual)
        result = jnp.einsum("abk,bk->ak", diag_blocks, precond, precision=lax.Precision.HIGHEST)
        result = result + band_by_sums(precond, masked)
        image_now = result + loop_apply(precond, local_tiles, row_ids, col_ids, live_count)
        gamma_now, delta_now = total_pair(jnp.sum(residual * precond), jnp.sum(precond * image_now))
        if iteration == 0:
            alpha_now = gamma_now / delta_now
            direction = precond
            along = image_now
        else:
            beta_now = gamma_now / gamma_old
            alpha_now = gamma_now / (delta_now - beta_now * gamma_now / alpha_old)
            direction = precond + beta_now * direction
            along = image_now + beta_now * along
        solution = solution + alpha_now * direction
        residual = residual - alpha_now * along
        gamma_old = gamma_now
        alpha_old = alpha_now
    return (solution, residual)


def solution(mesh):
    return jax.shard_map(
        per_device,
        mesh=mesh,
        in_specs=(
            P(None, ("frames", "cols")),
            P(None, None, ("frames", "cols")),
            P(None, None, None, ("frames", "cols")),
            P(("frames", "cols")),
            P("frames", "cols", None, None, None),
            P("frames", "cols", None),
            P("frames", "cols", None),
            P("frames", "cols"),
        ),
        out_specs=(P(None, ("frames", "cols")), P(None, ("frames", "cols"))),
        check_vma=False,
    )
```

profile of v0, /device:TPU:0, one launch (start us, length us, event | category | flops | bytes accessed | tf_op | source)
XLA Modules:
  0.0 735.6 jit_solution(5939563963265589089)
XLA Ops:
  7.2 0.8 fusion.199
  8.0 0.7 bitcast_subtract_fusion
  8.7 0.8 bitcast_subtract_fusion.1
  9.9 0.9 constant_dynamic-update-slice_fusion.5
  10.8 0.8 constant_dynamic-update-slice_fusion.4
  11.5 0.8 constant_dynamic-update-slice_fusion.3
  12.3 0.7 multiply_reduce_fusion.7
  13.0 6.2 all_gather.25
  19.2 31.3 %all_gather.24 = f32[6,2048]{1,0:T(8,128)S(1)} all-gather(f32[6,256]{1,0:T(8,128)S(1)} %bitcast.768), channel_id=1, replica_groups=mesh['frames'=8,'cols'=4] {'frames'}, dimensions={1}, use_global_device_ids=true | all-gather | bytes 55296 | tf_op jit(solution)/shard_map/all_gather | solution.py:63
  51.6 1.0 convolution_bitcast_fusion.14
  52.6 5.3 fusion.12
  58.1 4.4 fusion.14
  64.9 0.7 compare_reduce_fusion.4
  69.3 0.7 add_select_fusion.23
  70.3 0.8 add_select_fusion.22
  72.2 0.7 add_select_fusion.20
  75.3 1.3 collective-permute-start.1
  76.6 1.3 collective-permute-start
  78.3 0.7 reshape.3668
  79.4 2.0 collective-permute-done
  81.6 2.5 reduce-scatter.9.cloned.1.call-done
  84.1 65.1 %reduce-scatter.11.cloned.1.call-done = f32[6,256]{1,0:T(8,128)} async-done(((f32[6,2048]{1,0:T(8,128)}), f32[6,256]{1,0:T(8,128)}) %reduce-scatter.11.cloned.1.call-update) | async-done | bytes 6160 | tf_op jit(solution)/shard_map/reduce_scatter | solution.py:106
  149.2 1.4 multiply_reduce_fusion.14
  150.6 40.3 %all-reduce.11 = (f32[]{:T(128)}, f32[]{:T(128)}) all-reduce(f32[]{:T(128)} %get-tuple-element.529, f32[]{:T(128)} %get-tuple-element.528), channel_id=1, replica_groups=mesh['frames'=8,'cols'=4] {'frames','cols'}, use_global_device_ids=true, to_apply=%region_1.0 | all-reduce | flops 2 | bytes 16 | tf_op jit(solution)/shard_map/psum | solution.py:111
  192.3 5.8 all_gather.27
  198.1 30.7 %all_gather.26 = f32[6,2048]{1,0:T(8,128)S(1)} all-gather(f32[6,256]{1,0:T(8,128)S(1)} %bitcast.772), channel_id=1, replica_groups=mesh['frames'=8,'cols'=4] {'frames'}, dimensions={1}, use_global_device_ids=true | all-gather | bytes 55296 | tf_op jit(solution)/shard_map/all_gather | solution.py:63
  229.2 4.8 fusion.8
  234.4 6.6 fusion.10
  243.3 0.7 add_select_fusion.17
  244.3 0.8 add_select_fusion.16
  246.2 0.7 add_select_fusion.14
  249.6 1.3 collective-permute-start.2
  250.9 0.7 reshape.3674
  251.6 3.0 collective-permute-start.3
  255.4 4.9 reduce-scatter.13.cloned.1.call-done
  260.4 64.5 %reduce-scatter.15.cloned.1.call-done = f32[6,256]{1,0:T(8,128)} async-done(((f32[6,2048]{1,0:T(8,128)}), f32[6,256]{1,0:T(8,128)}) %reduce-scatter.15.cloned.1.call-update) | async-done | bytes 6160 | tf_op jit(solution)/shard_map/reduce_scatter | solution.py:106
  324.9 1.4 multiply_reduce_fusion.12
  326.3 40.4 %all-reduce.10 = (f32[]{:T(128)}, f32[]{:T(128)}) all-reduce(f32[]{:T(128)} %get-tuple-element.527, f32[]{:T(128)} %get-tuple-element.526), channel_id=1, replica_groups=mesh['frames'=8,'cols'=4] {'frames','cols'}, use_global_device_ids=true, to_apply=%region_14.15 | all-reduce | flops 2 | bytes 16 | tf_op jit(solution)/shard_map/psum | solution.py:111
  371.1 5.7 all_gather.29
  376.8 30.7 %all_gather.28 = f32[6,2048]{1,0:T(8,128)S(1)} all-gather(f32[6,256]{1,0:T(8,128)S(1)} %bitcast.776), channel_id=1, replica_groups=mesh['frames'=8,'cols'=4] {'frames'}, dimensions={1}, use_global_device_ids=true | all-gather | bytes 55296 | tf_op jit(solution)/shard_map/all_gather | solution.py:63
  407.9 4.8 fusion.4
  413.1 6.6 fusion.6
  422.1 0.7 add_select_fusion.11
  423.0 0.8 add_select_fusion.10
  428.3 1.3 collective-permute-start.4
  429.6 0.7 reshape.3680
  430.3 3.0 collective-permute-start.5
  434.2 4.9 reduce-scatter.17.cloned.1.call-done
  439.1 64.9 %reduce-scatter.19.cloned.1.call-done = f32[6,256]{1,0:T(8,128)} async-done(((f32[6,2048]{1,0:T(8,128)}), f32[6,256]{1,0:T(8,128)}) %reduce-scatter.19.cloned.1.call-update) | async-done | bytes 6160 | tf_op jit(solution)/shard_map/reduce_scatter | solution.py:106
  504.0 1.4 multiply_reduce_fusion.10
  505.4 40.3 %all-reduce.9 = (f32[]{:T(128)}, f32[]{:T(128)}) all-reduce(f32[]{:T(128)} %get-tuple-element.525, f32[]{:T(128)} %get-tuple-element.524), channel_id=1, replica_groups=mesh['frames'=8,'cols'=4] {'frames','cols'}, use_global_device_ids=true, to_apply=%region_20.21 | all-reduce | flops 2 | bytes 16 | tf_op jit(solution)/shard_map/psum | solution.py:111
  549.4 5.8 all_gather.31
  555.2 30.7 %all_gather.30 = f32[6,2048]{1,0:T(8,128)S(1)} all-gather(f32[6,256]{1,0:T(8,128)S(1)} %bitcast.780), channel_id=1, replica_groups=mesh['frames'=8,'cols'=4] {'frames'}, dimensions={1}, use_global_device_ids=true | all-gather | bytes 55296 | tf_op jit(solution)/shard_map/all_gather | solution.py:63
  586.4 4.8 fusion
  591.6 6.6 fusion.2
  600.5 0.7 add_select_fusion.5
  601.5 0.8 add_select_fusion.4
  606.8 1.3 collective-permute-start.6
  608.1 0.7 reshape.3686
  608.8 3.0 collective-permute-start.7
  612.7 5.0 reduce-scatter.21.cloned.1.call-done
  617.6 64.5 %reduce-scatter.23.cloned.1.call-done = f32[6,256]{1,0:T(8,128)} async-done(((f32[6,2048]{1,0:T(8,128)}), f32[6,256]{1,0:T(8,128)}) %reduce-scatter.23.cloned.1.call-update) | async-done | bytes 6160 | tf_op jit(solution)/shard_map/reduce_scatter | solution.py:106
  682.2 1.3 multiply_reduce_fusion.8
  683.5 40.5 %all-reduce.8 = (f32[]{:T(128)}, f32[]{:T(128)}) all-reduce(f32[]{:T(128)} %get-tuple-element.523, f32[]{:T(128)} %get-tuple-element.522), channel_id=1, replica_groups=mesh['frames'=8,'cols'=4] {'frames','cols'}, use_global_device_ids=true, to_apply=%region_26.27 | all-reduce | flops 2 | bytes 16 | tf_op jit(solution)/shard_map/psum | solution.py:111
  (222 shorter events, 37.7 us)
Async XLA Ops:
  7.2 50.7 %copy-start.6 = (s32[1,1,8]{2,1,0:T(1,128)S(1)}, s32[1,1,8]{2,1,0:T(1,128)}, u32[]{:S(2)}) copy-start(s32[1,1,8]{2,1,0:T(1,128)} %param.90) | copy-start | bytes 100
  7.2 77.0 %reduce-scatter.9.cloned.1.call-start = ((), (), s32[]{:S(2)}) async-start(), calls=%async_computation.8 | async-start | bytes 40960 | tf_op jit(solution)/shard_map/reduce_scatter | solution.py:105
  51.6 6.5 copy-start
  52.6 10.0 %copy-start.5 = (s32[1,1,8]{2,1,0:T(1,128)S(1)}, s32[1,1,8]{2,1,0:T(1,128)}, u32[]{:S(2)}) copy-start(s32[1,1,8]{2,1,0:T(1,128)} %param.89) | copy-start | bytes 100
  52.6 15.7 %copy-start.4 = (s32[256]{0:T(256)S(1)}, s32[256]{0:T(256)}, u32[]{:S(2)}) copy-start(s32[256]{0:T(256)} %param.87) | copy-start | bytes 3076
  52.6 15.8 %copy-start.2 = (f32[8,6,6,256]{3,0,2,1:T(8,128)S(1)}, f32[8,6,6,256]{3,0,2,1:T(8,128)}, u32[]{:S(2)}) copy-start(f32[8,6,6,256]{3,0,2,1:T(8,128)} %param.86) | copy-start | bytes 884740
  57.9 21.2 %copy-start.1 = (f32[6,6,256]{2,1,0:T(8,128)S(1)}, f32[6,6,256]{2,1,0:T(8,128)}, u32[]{:S(2)}) copy-start(f32[6,6,256]{2,1,0:T(8,128)} %param.85) | copy-start | bytes 110596
  57.9 91.4 %copy-start.3 = (f32[6,256]{1,0:T(8,128)S(1)}, f32[6,256]{1,0:T(8,128)}, u32[]{:S(2)}) copy-start(f32[6,256]{1,0:T(8,128)} %param.84) | copy-start | bytes 18436
  63.6 85.6 %reduce-scatter.11.cloned.1.call-start = ((), (), s32[]{:S(2)}) async-start(), calls=%async_computation.9 | async-start | bytes 73728 | tf_op jit(solution)/shard_map/reduce_scatter | solution.py:106
  75.3 6.4 collective-permute-start.1
  76.6 4.8 collective-permute-start
  79.0 181.4 %reduce-scatter.13.cloned.1.call-start = ((), (), s32[]{:S(2)}) async-start(), calls=%async_computation.10 | async-start | bytes 40960 | tf_op jit(solution)/shard_map/reduce_scatter | solution.py:105
  242.1 82.8 %reduce-scatter.15.cloned.1.call-start = ((), (), s32[]{:S(2)}) async-start(), calls=%async_computation.11 | async-start | bytes 73728 | tf_op jit(solution)/shard_map/reduce_scatter | solution.py:106
  249.6 5.1 collective-permute-start.2
  251.6 3.8 collective-permute-start.3
  254.7 184.4 %reduce-scatter.17.cloned.1.call-start = ((), (), s32[]{:S(2)}) async-start(), calls=%async_computation.12 | async-start | bytes 40960 | tf_op jit(solution)/shard_map/reduce_scatter | solution.py:105
  420.9 83.1 %reduce-scatter.19.cloned.1.call-start = ((), (), s32[]{:S(2)}) async-start(), calls=%async_computation.13 | async-start | bytes 73728 | tf_op jit(solution)/shard_map/reduce_scatter | solution.py:106
  428.3 5.1 collective-permute-start.4
  430.3 3.8 collective-permute-start.5
  433.4 184.2 %reduce-scatter.21.cloned.1.call-start = ((), (), s32[]{:S(2)}) async-start(), calls=%async_computation.14 | async-start | bytes 40960 | tf_op jit(solution)/shard_map/reduce_scatter | solution.py:105
  599.4 82.8 %reduce-scatter.23.cloned.1.call-start = ((), (), s32[]{:S(2)}) async-start(), calls=%async_computation.15 | async-start | bytes 73728 | tf_op jit(solution)/shard_map/reduce_scatter | solution.py:106
  606.8 5.1 collective-permute-start.6
  608.8 3.8 collective-permute-start.7
Sparse Core Ops, SparseCore 0:
  63.7 20.3 reduce-scatter.8
  87.9 61.2 reduce-scatter.10
  242.3 18.0 reduce-scatter.12
  263.6 61.2 reduce-scatter.14
  421.0 18.0 reduce-scatter.16
  442.7 61.2 reduce-scatter.18
  599.5 18.1 reduce-scatter.20
  621.0 61.0 reduce-scatter.22
where the time goes:
time: 746 us; the launch traced here: 736 us
  blocking collectives  308 us (41%)
  waiting for transfers between devices  280 us (38%)
  matrix products  48.6 us (7%)
  other arithmetic  37 us (5%)
  between operations  29 us (4%)
  local copies, waits for them, and re-layouts  16.9 us (2%)
  starting transfers between devices  15.8 us (2%)
    reduce_scatter x4, waiting for transfers between devices, loop_apply(): lax.psum_scatter(col_acc, 'frames', scatter_dimension=1, tiled=True)  259 us
    psum x4, blocking collectives, total_pair(): return lax.psum((first, second), ('frames', 'cols'))  161 us
    all_gather x4, blocking collectives, loop_apply(): col_group = lax.all_gather(vector, 'frames', axis=1, tiled=True)  123 us
    another operation x35, other arithmetic  24.2 us
    dot_general x4, matrix products, loop_apply(): jnp.einsum('skn,sn->sk', local_tiles, col_pieces, precision=lax.Precision...  24.2 us
    all_gather x4, blocking collectives, loop_apply(): row_group = lax.all_gather(vector, 'cols', axis=1, tiled=True)  23.5 us
    dot_general x4, matrix products, loop_apply(): jnp.einsum('sk,skn->sn', row_pieces, local_tiles, precision=lax.Precision...  19.7 us
    reduce_scatter x4, waiting for transfers between devices, loop_apply(): lax.psum_scatter(row_acc, 'cols', scatter_dimension=1, tiled=True)  17.3 us
  transfers between devices with their start and end apart: 16, of which 12 were waited for; matrix products, arithmetic and copies ran while one was open for 5% of the time, Pallas kernels for 0%

commit v1 on v0

v1 whole, which is shorter than its diff:
```python
import functools

import jax
import jax.numpy as jnp
from jax import lax
from jax.experimental import pallas as pl
from jax.experimental.pallas import tpu as pltpu
from jax.sharding import PartitionSpec as P

ITERS = 4
COMP = 6
SUB = 8
MESH = pl.DeviceIdType.MESH
HIGH = lax.Precision.HIGHEST


def swap_pairs(block, side):
    row = lax.broadcasted_iota(jnp.int32, block.shape, 0)
    lane = lax.broadcasted_iota(jnp.int32, block.shape, 1)
    odd = row % 2
    turned = pltpu.roll(block, side, 1)
    above = pltpu.roll(turned, SUB - 1, 0)
    below = pltpu.roll(turned, 1, 0)
    return jnp.where(odd == lane // side, block, jnp.where(odd == 0, above, below))


def kernel(
    nf,
    nc,
    rhs_ref,
    diag_ref,
    band_ref,
    reach_ref,
    tiles_hbm,
    rows_ref,
    cols_ref,
    count_ref,
    sol_ref,
    res_ref,
    tiles,
    band,
    inv,
    vecs,
    ys,
    row_in,
    col_in,
    halo_in,
    spill_out,
    spill_in,
    row_out,
    col_out,
    row_back,
    col_back,
    last_out,
    last_in,
    pick_row,
    pick_col,
    put_row,
    put_col,
    r_cols,
    c_rows,
    g_cols,
    col_acc,
    nus,
    tile_sem,
    s_row,
    r_row,
    s_col,
    r_col,
    s_halo,
    r_halo,
    s_spill,
    r_spill,
    s_rowb,
    r_rowb,
    s_colb,
    r_colb,
    s_last,
    r_last,
):
    f = lax.axis_index("frames")
    c = lax.axis_index("cols")
    slots, tile, _ = tiles.shape
    side = tile // COMP
    lanes = 2 * side
    chunks = tile // lanes
    blocks = vecs.shape[1]
    frames = blocks * lanes
    slab = blocks * SUB
    reach_len = band_ref.shape[0]

    load = pltpu.make_async_copy(tiles_hbm.at[0, 0], tiles, tile_sem)
    load.start()

    row_peers = [(f, lax.rem(c + d, nc)) for d in range(1, nc)]
    col_peers = [(lax.rem(f + d, nf), c) for d in range(1, nf)]
    after = (lax.rem(f + (c + 1) // nc, nf), lax.rem(c + 1, nc))
    before = (lax.rem(f + nf - 1 + (c + nc - 1) // nc, nf), lax.rem(c + nc - 1, nc))
    greet = row_peers + col_peers + [after, before]
    barrier = pltpu.get_barrier_semaphore()
    for peer in greet:
        pl.semaphore_signal(barrier, inc=1, device_id=peer, device_id_type=MESH)

    row_iota = lax.broadcasted_iota(jnp.int32, (SUB, lanes), 0)
    lane_iota = lax.broadcasted_iota(jnp.int32, (SUB, lanes), 1)
    zero = jnp.zeros((SUB, lanes), jnp.float32)

    ys[0] = jnp.zeros((blocks, SUB, lanes), jnp.float32)
    inv[...] = jnp.zeros_like(inv)
    band[...] = jnp.zeros_like(band)
    for h in range(blocks):
        cut = slice(h * lanes, (h + 1) * lanes)
        ys[0, h, 0:COMP, :] = rhs_ref[:, cut]
        for a in range(COMP):
            inv[a, h, 0:COMP, :] = diag_ref[a, :, cut]
    for h in range(blocks):
        mat = [inv[a, h] for a in range(COMP)]
        out = [jnp.where(row_iota == a, 1.0, 0.0) for a in range(COMP)]
        for p in range(COMP):
            pivot = mat[p][p : p + 1, :]
            mat[p] = mat[p] / pivot
            out[p] = out[p] / pivot
            for a in range(COMP):
                if a != p:
                    factor = mat[a][p : p + 1, :]
                    mat[a] = mat[a] - factor * mat[p]
                    out[a] = out[a] - factor * out[p]
        for a in range(COMP):
            inv[a, h] = out[a]

    def precondition(h, value):
        total = zero
        for a in range(COMP):
            total = total + inv[a, h] * value[a : a + 1, :]
        return total

    for h in range(blocks):
        vecs[0, h] = precondition(h, ys[0, h])

    ends = (f == nf - 1) & (c == nc - 1)
    limit = jnp.where(ends, frames, frames + reach_len)
    for h in range(blocks):
        cut = slice(h * lanes, (h + 1) * lanes)
        reach = reach_ref[:, cut]
        at = lax.broadcasted_iota(jnp.int32, (1, lanes), 1) + h * lanes
        for o in range(1, reach_len + 1):
            keep = jnp.where((o <= reach) & (at + o < limit), 1.0, 0.0)
            for a in range(COMP):
                band[o - 1, a, h, 0:COMP, :] = band_ref[o - 1, a, :, cut] * keep

    count = count_ref[0, 0]

    def targets(ids_ref, iota, width):
        out = jnp.full(iota.shape, -1, jnp.int32)
        slot_at = iota // width
        for s in range(slots):
            at = ids_ref[0, 0, s]
            base = jnp.where(s < count, (at // 2) * SUB + lax.rem(at, 2), -slab * nf * nc)
            for j in range(chunks):
                out = jnp.where(slot_at == j * slots + s, base + 2 * j, out)
        return out

    for ids, pick, put, width in ((rows_ref, pick_row, put_row, 1), (cols_ref, pick_col, put_col, SUB)):
        many = pick.shape[1]
        down = targets(ids, lax.broadcasted_iota(jnp.int32, (pick.shape[0], 1), 0), 1)
        pick[...] = jnp.where(lax.broadcasted_iota(jnp.int32, pick.shape, 1) == down, 1.0, 0.0)
        along = targets(ids, lax.broadcasted_iota(jnp.int32, (1, put.shape[1]), 1), width)
        put[...] = jnp.where(lax.broadcasted_iota(jnp.int32, put.shape, 0) == along, 1.0, 0.0)

    pl.semaphore_wait(barrier, len(greet))

    def remote(src, dst, send, recv, peer):
        copy = pltpu.make_async_remote_copy(
            src_ref=src, dst_ref=dst, send_sem=send, recv_sem=recv, device_id=peer, device_id_type=MESH
        )
        copy.start()
        return copy

    def step(k, carry):
        prev = jnp.maximum(k - 1, 0)
        v = [vecs[k, h] for h in range(blocks)]
        even = jnp.zeros((1, lanes), jnp.float32)
        odd = jnp.zeros((1, lanes), jnp.float32)
        for h in range(blocks):
            y = ys[k, h]
            even = even + jnp.sum(v[h] * y, axis=0, keepdims=True)
            odd = odd + jnp.sum(vecs[prev, h] * y, axis=0, keepdims=True)
        paired = [swap_pairs(v[h], side) for h in range(blocks)]
        paired[0] = jnp.where(row_iota == COMP, even, jnp.where(row_iota == COMP + 1, odd, paired[0]))
        for h in range(blocks):
            row_in[k, c, h * SUB : (h + 1) * SUB, :] = paired[h]
            col_in[k, f, h * SUB : (h + 1) * SUB, :] = paired[h]
        gathers = []
        for d in range(1, nf):
            gathers.append(remote(col_in.at[k, f], col_in.at[k, f], s_col.at[k, d], r_col.at[k, d], col_peers[d - 1]))
        for d in range(1, nc):
            gathers.append(remote(row_in.at[k, c], row_in.at[k, c], s_row.at[k, d], r_row.at[k, d], row_peers[d - 1]))
        halo = remote(vecs.at[k, 0], halo_in.at[k], s_halo.at[k], r_halo.at[k], before)

        image = [zero] * blocks
        spill = zero
        for o in range(1, reach_len + 1):
            passed = zero
            for h in range(blocks):
                term = zero
                for a in range(COMP):
                    term = term + band[o - 1, a, h] * v[h][a : a + 1, :]
                turned = pltpu.roll(term, o, 1)
                image[h] = image[h] + jnp.where(lane_iota >= o, turned, passed)
                passed = turned
            spill = spill + jnp.where(lane_iota < o, passed, 0.0)
        spill_out[k] = spill
        spilled = remote(spill_out.at[k], spill_in.at[k], s_spill.at[k], r_spill.at[k], after)

        halo.wait_recv()
        ext = v + [halo_in[k]]
        forward = [[zero] * COMP for _ in range(blocks)]
        for o in range(1, reach_len + 1):
            turned = [pltpu.roll(part, lanes - o, 1) for part in ext]
            for h in range(blocks):
                moved = jnp.where(lane_iota < lanes - o, turned[h], turned[h + 1])
                for a in range(COMP):
                    forward[h][a] = forward[h][a] + band[o - 1, a, h] * moved
        quad = jnp.zeros((1, lanes), jnp.float32)
        for h in range(blocks):
            ahead = zero
            for a in range(COMP):
                ahead = jnp.where(row_iota == a, jnp.sum(forward[h][a], axis=0, keepdims=True), ahead)
            quad = quad + jnp.sum(ahead * v[h], axis=0, keepdims=True)
            image[h] = image[h] + ahead

        for copy in gathers:
            copy.wait_recv()
        rows_all = row_in[k].reshape(nc * slab, lanes)
        cols_all = col_in[k].reshape(nf * slab, lanes)
        r_cols[...] = jnp.dot(pick_row[...], rows_all, precision=HIGH, preferred_element_type=jnp.float32).T
        c_rows[...] = jnp.dot(pick_col[...], cols_all, precision=HIGH, preferred_element_type=jnp.float32)

        @pl.when(k == 0)
        def _():
            load.wait()

        def strip(i, accs):
            accs = list(accs)
            at = pl.multiple_of(i * SUB, SUB)
            r_now = r_cols[pl.ds(at, SUB), :]
            g_now = zero
            for s in range(slots):
                for j in range(chunks):
                    col = j * slots + s
                    spot = pl.multiple_of(j * lanes + at, SUB)
                    x = jnp.broadcast_to(r_now[:, col : col + 1], (SUB, lanes))
                    dots = zero
                    for n in range(chunks):
                        part = tiles[s, pl.ds(spot, SUB), n * lanes : (n + 1) * lanes]
                        here = n * slots + s
                        dots = dots + part * c_rows[here : here + 1, :]
                        accs[here] = accs[here] + part * x
                    g_now = jnp.where(lane_iota == col, jnp.sum(dots, axis=1, keepdims=True), g_now)
            g_cols[pl.ds(at, SUB), :] = g_now
            return tuple(accs)

        accs = lax.fori_loop(0, lanes // SUB, strip, (zero,) * (slots * chunks))
        for q in range(slots * chunks):
            col_acc[q * SUB : (q + 1) * SUB, :] = accs[q]
        gains = g_cols[...]
        quad = 2.0 * (quad + jnp.sum(gains * r_cols[...], axis=0, keepdims=True))
        row_out[k] = jnp.dot(put_row[...], gains.T, precision=HIGH, preferred_element_type=jnp.float32)
        col_out[k] = jnp.dot(put_col[...], col_acc[...], precision=HIGH, preferred_element_type=jnp.float32)
        sums = jnp.zeros((2, lanes), jnp.float32)
        for d in range(nc):
            sums = sums + row_in[k, d, COMP:SUB, :]
        for d in range(nf):
            col_out[k, d * slab + COMP : d * slab + SUB, :] = sums
        for d in range(nc):
            spot = (d + 1) * slab - SUB + COMP
            row_out[k, spot : spot + 1, :] = quad
        backs = []
        for d in range(1, nf):
            peer = col_peers[d - 1]
            part = col_out.at[k, pl.ds(pl.multiple_of(peer[0] * slab, SUB), slab), :]
            backs.append(remote(part, col_back.at[k, f], s_colb.at[k, d], r_colb.at[k, d], peer))
        for d in range(1, nc):
            peer = row_peers[d - 1]
            part = row_out.at[k, pl.ds(pl.multiple_of(peer[1] * slab, SUB), slab), :]
            backs.append(remote(part, row_back.at[k, c], s_rowb.at[k, d], r_rowb.at[k, d], peer))
        col_back[k, f] = col_out[k, pl.ds(pl.multiple_of(f * slab, SUB), slab), :]
        row_back[k, c] = row_out[k, pl.ds(pl.multiple_of(c * slab, SUB), slab), :]
        spilled.wait_recv()
        image[0] = image[0] + spill_in[k]
        for copy in backs:
            copy.wait_recv()
        total = jnp.sum(row_back[k], axis=0) + jnp.sum(col_back[k], axis=0)
        nus[k] = total
        for h in range(blocks):
            part = jnp.where(row_iota < COMP, total[h * SUB : (h + 1) * SUB, :], 0.0)
            image[h] = image[h] + swap_pairs(part, side)
            ys[k + 1, h] = image[h]
            vecs[k + 1, h] = precondition(h, image[h])
        for copy in gathers + [halo, spilled] + backs:
            copy.wait_send()
        return carry

    lax.fori_loop(0, ITERS, step, 0)

    last = ITERS - 1
    last_out[...] = nus[last, slab - SUB : slab, :]
    finals = []
    for d in range(1, nf):
        finals.append(remote(last_out, last_in.at[f], s_last.at[d], r_last.at[d], col_peers[d - 1]))
    last_in[f] = last_out[...]

    moments = []
    for k in range(ITERS):
        if k:
            moments.append(jnp.sum(nus[k, COMP + 1 : COMP + 2, :], axis=1, keepdims=True))
        moments.append(jnp.sum(nus[k, COMP : COMP + 1, :], axis=1, keepdims=True))

    def quadratic(coefs, values):
        sums = {}
        for i, left in enumerate(coefs):
            for j, right in enumerate(coefs):
                sums.setdefault(i + j, []).append(left * right)
        total = None
        for at, terms in sums.items():
            term = sum(terms[1:], terms[0]) * values(at)
            total = term if total is None else total + term
        return total

    one = jnp.ones((1, 1), jnp.float32)
    none = jnp.zeros((1, 1), jnp.float32)
    rho = [one]
    pi = [one]
    xi = []
    gamma = quadratic(rho, lambda at: moments[at])
    for iteration in range(ITERS):
        if iteration == last:
            for copy in finals:
                copy.wait_recv()
            ending = jnp.sum(last_in[...], axis=0)[COMP : COMP + 1, :]
            moments.append(jnp.sum(ending, axis=1, keepdims=True))
        alpha = gamma / quadratic(pi, lambda at: moments[at] + moments[at + 1])
        xi = [x + alpha * p for x, p in zip(xi + [none] * (len(pi) - len(xi)), pi)]
        image = [(pi[i] if i < len(pi) else none) + (pi[i - 1] if i else none) for i in range(len(pi) + 1)]
        rho = [r - alpha * s for r, s in zip(rho + [none], image)]
        if iteration < last:
            fresh = quadratic(rho, lambda at: moments[at])
            beta = fresh / gamma
            pi = [r + beta * p for r, p in zip(rho, pi + [none])]
            gamma = fresh

    for h in range(blocks):
        cut = slice(h * lanes, (h + 1) * lanes)
        sol = zero
        res = zero
        for k in range(ITERS):
            sol = sol + xi[k] * vecs[k, h]
        for k in range(ITERS + 1):
            res = res + rho[k] * ys[k, h]
        sol_ref[:, cut] = sol[0:COMP, :]
        res_ref[:, cut] = res[0:COMP, :]
    for copy in finals:
        copy.wait_send()


def per_device(nf, nc, right_side, diag_blocks, band_blocks, reach, tiles, tile_rows, tile_cols, tile_count):
    slots, tile = tiles.shape[2], tiles.shape[3]
    lanes = 2 * (tile // COMP)
    chunks = tile // lanes
    frames = right_side.shape[1]
    blocks = frames // lanes
    slab = blocks * SUB
    reach_len = band_blocks.shape[0]
    padded = -(-slots * chunks // lanes) * lanes
    f32 = jnp.float32
    vmem = pl.BlockSpec(memory_space=pltpu.VMEM)
    smem = pl.BlockSpec(memory_space=pltpu.SMEM)
    dma = pltpu.SemaphoreType.DMA
    scratch = [
        pltpu.VMEM((slots, tile, tile), f32),
        pltpu.VMEM((reach_len, COMP, blocks, SUB, lanes), f32),
        pltpu.VMEM((COMP, blocks, SUB, lanes), f32),
        pltpu.VMEM((ITERS + 1, blocks, SUB, lanes), f32),
        pltpu.VMEM((ITERS + 1, blocks, SUB, lanes), f32),
        pltpu.VMEM((ITERS, nc, slab, lanes), f32),
        pltpu.VMEM((ITERS, nf, slab, lanes), f32),
        pltpu.VMEM((ITERS, SUB, lanes), f32),
        pltpu.VMEM((ITERS, SUB, lanes), f32),
        pltpu.VMEM((ITERS, SUB, lanes), f32),
        pltpu.VMEM((ITERS, nc * slab, lanes), f32),
        pltpu.VMEM((ITERS, nf * slab, lanes), f32),
        pltpu.VMEM((ITERS, nc, slab, lanes), f32),
        pltpu.VMEM((ITERS, nf, slab, lanes), f32),
        pltpu.VMEM((SUB, lanes), f32),
        pltpu.VMEM((nf, SUB, lanes), f32),
        pltpu.VMEM((padded, nc * slab), f32),
        pltpu.VMEM((padded, nf * slab), f32),
        pltpu.VMEM((nc * slab, padded), f32),
        pltpu.VMEM((nf * slab, slots * chunks * SUB), f32),
        pltpu.VMEM((lanes, padded), f32),
        pltpu.VMEM((padded, lanes), f32),
        pltpu.VMEM((lanes, padded), f32),
        pltpu.VMEM((slots * chunks * SUB, lanes), f32),
        pltpu.VMEM((ITERS, slab, lanes), f32),
        dma,
    ]
    for shape in ((ITERS, nc), (ITERS, nf), (ITERS,), (ITERS,), (ITERS, nc), (ITERS, nf), (nf,)):
        scratch += [dma(shape), dma(shape)]
    return pl.pallas_call(
        functools.partial(kernel, nf, nc),
        out_shape=(jax.ShapeDtypeStruct(right_side.shape, f32), jax.ShapeDtypeStruct(right_side.shape, f32)),
        in_specs=[vmem, vmem, vmem, vmem, pl.BlockSpec(memory_space=pl.ANY), smem, smem, smem],
        out_specs=(vmem, vmem),
        scratch_shapes=scratch,
        compiler_params=pltpu.CompilerParams(
            collective_id=0, has_side_effects=True, vmem_limit_bytes=32 * 1024 * 1024
        ),
        cost_estimate=pl.CostEstimate(
            flops=4 * ITERS * tiles.size, bytes_accessed=4 * (tiles.size + band_blocks.size), transcendentals=0
        ),
    )(right_side, diag_blocks, band_blocks, reach.reshape(1, -1), tiles, tile_rows, tile_cols, tile_count)


def solution(mesh):
    return jax.shard_map(
        functools.partial(per_device, mesh.shape["frames"], mesh.shape["cols"]),
        mesh=mesh,
        in_specs=(
            P(None, ("frames", "cols")),
            P(None, None, ("frames", "cols")),
            P(None, None, None, ("frames", "cols")),
            P(("frames", "cols")),
            P("frames", "cols", None, None, None),
            P("frames", "cols", None),
            P("frames", "cols", None),
            P("frames", "cols"),
        ),
        out_specs=(P(None, ("frames", "cols")), P(None, ("frames", "cols"))),
        check_vma=False,
    )
```

time: 746 us -> 84.6 us (0.11); the launches traced: 736 us -> 84.3 us
  blocking collectives: 308 us -> 0 us
  waiting for transfers between devices: 280 us -> 0 us
  Pallas kernels: 0 us -> 74.9 us
  matrix products: 48.6 us -> 0 us
  other arithmetic: 37 us -> 0 us
  between operations: 29 us -> 1.3 us
  starting transfers between devices: 15.8 us -> 0 us
  local copies, waits for them, and re-layouts: 16.9 us -> 8.08 us
    reduce_scatter x8 -> x0, waiting for transfers between devices: 276 us -> none  [the longest x4 259 us: loop_apply(): lax.psum_scatter(col_acc, 'frames', scatter_dimension=1, tiled=True)]
    psum x4 -> x0, blocking collectives: 161 us -> none  [total_pair(): return lax.psum((first, second), ('frames', 'cols'))]
    all_gather x8 -> x0, blocking collectives: 147 us -> none  [the longest x4 123 us: loop_apply(): col_group = lax.all_gather(vector, 'frames', axis=1, tiled=True)]
    pallas_call x0 -> x1, Pallas kernels: none -> 74.9 us  [per_device(): pl.pallas_call(functools.partial(kernel, nf, nc), out_shape=(jax.ShapeDty...]
    dot_general x24 -> x0, matrix products: 48.6 us -> none  [the longest x4 24.2 us: loop_apply(): jnp.einsum('skn,sn->sk', local_tiles, col_pieces, precision=lax.Precision...]
    another operation x35 -> x0, other arithmetic: 24.2 us -> none
    ppermute x8 -> x0, starting transfers between devices: 15.5 us -> none  [shifted(): lax.ppermute(value, axis, [(source, source + steps) for source in range(i...]
    unnamed x14 -> x15, local copies, waits for them, and re-layouts: 0.03 us -> 8.08 us
  transfers between devices with their start and end apart: 16 -> 0, of which waited for: 12 -> 0; matrix products, arithmetic and copies ran while one was open for 5% -> 0% of each run, Pallas kernels for 0% -> 0%
where the time goes in v1:
time: 84.6 us; the launch traced here: 84.3 us
  Pallas kernels  74.9 us (89%)
  local copies, waits for them, and re-layouts  8.08 us (10%)
  between operations  1.3 us (2%)
    pallas_call x1, Pallas kernels, per_device(): pl.pallas_call(functools.partial(kernel, nf, nc), out_shape=(jax.ShapeDty...  74.9 us
    unnamed x15, local copies, waits for them, and re-layouts  8.08 us

profile of v1, /device:TPU:0, one launch (start us, length us, event | category | flops | bytes accessed | tf_op | source)
XLA Modules:
  0.0 84.3 jit_solution(3755689163254196826)
XLA Ops:
  1.3 1.1 %copy.10.band_ref = f32[8,6,6,256]{3,2,1,0:T(8,128)S(1)} copy(f32[8,6,6,256]{3,0,2,1:T(8,128)} %param.10) | data formatting | bytes 589824 | tf_op args[2]
  2.3 0.0 copy-start
  2.4 2.3 %copy-done = f32[1,1,8,384,384]{4,3,2,1,0:T(8,128)S(1)} copy-done((f32[1,1,8,384,384]{4,3,2,1,0:T(8,128)S(1)}, f32[1,1,8,384,384]{4,3,2,1,0:T(8,128)}, u32[]{:S(2)}) %copy-start) | copy-done | bytes 4718616
  4.7 0.0 copy-start.1
  4.7 0.8 copy-done.1
  5.5 0.0 copy-start.2
  5.5 0.7 copy-done.2
  6.2 0.0 copy-start.3
  6.2 0.7 copy-done.3
  6.9 0.0 copy-start.4
  6.9 0.7 copy-done.4
  7.5 0.0 copy-start.5
  7.5 0.7 copy-done.5
  8.2 74.9 %shard_map.95 = (f32[6,256]{1,0:T(8,128)S(1)}, f32[6,256]{1,0:T(8,128)S(1)}) custom-call(f32[6,256]{1,0:T(8,128)S(1)} %copy-done.2, f32[6,6,256]{2,1,0:T(8,128)S(1)} %copy-done.1, f32[8,6,6,256]{3,2,1,0:T(8,128)S(1)} %copy.10.band_ref, s32[1,256]{1,0:T(1,128)S(1)} %bitcast.1, f32[1,1,8,384,384]{4,3,2,1,0:T(8,128)S(1)} %copy-done, s32[1,1,8]{2,1,0:T(1,128)S(1)} %copy-done.4, ...), custom_call_target="tpu_custom_call" | custom-call | flops 18874368 | bytes 5013504 | tf_op jit(solution)/shard_map/pallas_call | solution.py:409
  83.1 0.6 copy.14
  83.7 0.6 copy.15
Async XLA Ops:
  2.3 2.3 %copy-start = (f32[1,1,8,384,384]{4,3,2,1,0:T(8,128)S(1)}, f32[1,1,8,384,384]{4,3,2,1,0:T(8,128)}, u32[]{:S(2)}) copy-start(f32[1,1,8,384,384]{4,3,2,1,0:T(8,128)} %tiles_hbm.1) | copy-start | bytes 14155780
  4.7 0.8 copy-start.1
  5.5 0.7 copy-start.2
  6.2 0.7 copy-start.3
  6.9 0.7 copy-start.4
  7.5 0.7 copy-start.5

commit v2 on v1

--- a/solution.py
+++ b/solution.py
@@ -10,8 +10,8 @@
 ITERS = 4
 COMP = 6
 SUB = 8
+UNROLL = 4
 MESH = pl.DeviceIdType.MESH
-HIGH = lax.Precision.HIGHEST
 
 
 def swap_pairs(block, side):
@@ -24,21 +24,38 @@
     return jnp.where(odd == lane // side, block, jnp.where(odd == 0, above, below))
 
 
+def flip_rows(block):
+    row = lax.broadcasted_iota(jnp.int32, block.shape, 0)
+    block = pltpu.roll(block, SUB // 2, 0)
+    for step in (2, 1):
+        up, down = pltpu.roll(block, SUB - step, 0), pltpu.roll(block, step, 0)
+        block = jnp.where((row // step) % 2 == 0, up, down)
+    return block
+
+
 def kernel(
     nf,
     nc,
+    rhs_hbm,
+    diag_hbm,
+    band_hbm,
+    reach_hbm,
+    tiles_hbm,
+    rows_hbm,
+    cols_hbm,
+    count_hbm,
+    sol_ref,
+    res_ref,
     rhs_ref,
     diag_ref,
     band_ref,
     reach_ref,
-    tiles_hbm,
     rows_ref,
     cols_ref,
     count_ref,
-    sol_ref,
-    res_ref,
     tiles,
     band,
+    flipped,
     inv,
     vecs,
     ys,
@@ -60,9 +77,9 @@
     r_cols,
     c_rows,
     g_cols,
-    col_acc,
     nus,
     tile_sem,
+    load_sem,
     s_row,
     r_row,
     s_col,
@@ -87,8 +104,24 @@
     blocks = vecs.shape[1]
     frames = blocks * lanes
     slab = blocks * SUB
-    reach_len = band_ref.shape[0]
-
+    reach_len = band_ref.shape[2]
+
+    small = [
+        pltpu.make_async_copy(src, dst, load_sem.at[at])
+        for at, (src, dst) in enumerate(
+            (
+                (diag_hbm, diag_ref),
+                (rhs_hbm, rhs_ref),
+                (rows_hbm, rows_ref),
+                (cols_hbm, cols_ref),
+                (count_hbm, count_ref),
+                (reach_hbm, reach_ref),
+                (band_hbm, band_ref),
+            )
+        )
+    ]
+    for copy in small:
+        copy.start()
     load = pltpu.make_async_copy(tiles_hbm.at[0, 0], tiles, tile_sem)
     load.start()
 
@@ -107,7 +140,8 @@
 
     ys[0] = jnp.zeros((blocks, SUB, lanes), jnp.float32)
     inv[...] = jnp.zeros_like(inv)
-    band[...] = jnp.zeros_like(band)
+    for copy in small:
+        copy.wait()
     for h in range(blocks):
         cut = slice(h * lanes, (h + 1) * lanes)
         ys[0, h, 0:COMP, :] = rhs_ref[:, cut]
@@ -141,12 +175,14 @@
     limit = jnp.where(ends, frames, frames + reach_len)
     for h in range(blocks):
         cut = slice(h * lanes, (h + 1) * lanes)
-        reach = reach_ref[:, cut]
-        at = lax.broadcasted_iota(jnp.int32, (1, lanes), 1) + h * lanes
-        for o in range(1, reach_len + 1):
-            keep = jnp.where((o <= reach) & (at + o < limit), 1.0, 0.0)
-            for a in range(COMP):
-                band[o - 1, a, h, 0:COMP, :] = band_ref[o - 1, a, :, cut] * keep
+        offset = row_iota + 1
+        keep = (offset <= reach_ref[:, cut]) & (lane_iota + h * lanes + offset < limit)
+        keep = jnp.where(keep, 1.0, 0.0)
+        for a in range(COMP):
+            for b in range(COMP):
+                block = band_ref[a, b, :, cut] * keep
+                band[a, b, h] = block
+                flipped[a, b, h] = flip_rows(block)
 
     count = count_ref[0, 0]
 
@@ -161,11 +197,14 @@
         return out
 
     for ids, pick, put, width in ((rows_ref, pick_row, put_row, 1), (cols_ref, pick_col, put_col, SUB)):
-        many = pick.shape[1]
-        down = targets(ids, lax.broadcasted_iota(jnp.int32, (pick.shape[0], 1), 0), 1)
-        pick[...] = jnp.where(lax.broadcasted_iota(jnp.int32, pick.shape, 1) == down, 1.0, 0.0)
-        along = targets(ids, lax.broadcasted_iota(jnp.int32, (1, put.shape[1]), 1), width)
-        put[...] = jnp.where(lax.broadcasted_iota(jnp.int32, put.shape, 0) == along, 1.0, 0.0)
+        rows, wide = pick.shape[0], pick.shape[1] // 3
+        down = targets(ids, lax.broadcasted_iota(jnp.int32, (rows, 1), 0), 1)
+        once = jnp.where(lax.broadcasted_iota(jnp.int32, (rows, wide), 1) == down, 1.0, 0.0)
+        pick[...] = jnp.concatenate([once] * 3, axis=1).astype(jnp.bfloat16)
+        rows, wide = put.shape[0], put.shape[1] // 3
+        along = targets(ids, lax.broadcasted_iota(jnp.int32, (1, wide), 1), width)
+        once = jnp.where(lax.broadcasted_iota(jnp.int32, (rows, wide), 0) == along, 1.0, 0.0)
+        put[...] = jnp.concatenate([once] * 3, axis=1).astype(jnp.bfloat16)
 
     pl.semaphore_wait(barrier, len(greet))
 
@@ -175,6 +214,14 @@
         )
         copy.start()
         return copy
+
+    def select(pick, value):
+        first = value.astype(jnp.bfloat16)
+        left = value - first.astype(jnp.float32)
+        second = left.astype(jnp.bfloat16)
+        third = (left - second.astype(jnp.float32)).astype(jnp.bfloat16)
+        parts = jnp.concatenate([first, second, third], axis=0)
+        return jnp.dot(pick[...], parts, preferred_element_type=jnp.float32)
 
     def step(k, carry):
         prev = jnp.maximum(k - 1, 0)
@@ -190,37 +237,80 @@
         for h in range(blocks):
             row_in[k, c, h * SUB : (h + 1) * SUB, :] = paired[h]
             col_in[k, f, h * SUB : (h + 1) * SUB, :] = paired[h]
-        gathers = []
+        row_gets, col_gets = [], []
         for d in range(1, nf):
-            gathers.append(remote(col_in.at[k, f], col_in.at[k, f], s_col.at[k, d], r_col.at[k, d], col_peers[d - 1]))
+            col_gets.append(remote(col_in.at[k, f], col_in.at[k, f], s_col.at[k, d], r_col.at[k, d], col_peers[d - 1]))
         for d in range(1, nc):
-            gathers.append(remote(row_in.at[k, c], row_in.at[k, c], s_row.at[k, d], r_row.at[k, d], row_peers[d - 1]))
+            row_gets.append(remote(row_in.at[k, c], row_in.at[k, c], s_row.at[k, d], r_row.at[k, d], row_peers[d - 1]))
         halo = remote(vecs.at[k, 0], halo_in.at[k], s_halo.at[k], r_halo.at[k], before)
 
         image = [zero] * blocks
         spill = zero
-        for o in range(1, reach_len + 1):
+        for b in range(COMP):
             passed = zero
             for h in range(blocks):
                 term = zero
                 for a in range(COMP):
-                    term = term + band[o - 1, a, h] * v[h][a : a + 1, :]
-                turned = pltpu.roll(term, o, 1)
-                image[h] = image[h] + jnp.where(lane_iota >= o, turned, passed)
+                    term = term + band[a, b, h] * v[h][a : a + 1, :]
+                turned = pltpu.roll(term, 1, 1, stride=1, stride_axis=0)
+                moved = jnp.sum(jnp.where(lane_iota > row_iota, turned, passed), axis=0, keepdims=True)
+                image[h] = jnp.where(row_iota == b, moved, image[h])
                 passed = turned
-            spill = spill + jnp.where(lane_iota < o, passed, 0.0)
+            moved = jnp.sum(jnp.where(lane_iota > row_iota, 0.0, passed), axis=0, keepdims=True)
+            spill = jnp.where(row_iota == b, moved, spill)
         spill_out[k] = spill
         spilled = remote(spill_out.at[k], spill_in.at[k], s_spill.at[k], r_spill.at[k], after)
+
+        for copy in row_gets:
+            copy.wait_recv()
+        rows_all = row_in[k].reshape(nc * slab, lanes)
+        r_cols[...] = select(pick_row, rows_all).T
+
+        @pl.when(k == 0)
+        def _():
+            load.wait()
+
+        def transposed(i, accs):
+            accs = list(accs)
+            for u in range(UNROLL):
+                at = pl.multiple_of(i * (SUB * UNROLL) + u * SUB, SUB)
+                r_now = r_cols[pl.ds(at, SUB), :]
+                for s in range(slots):
+                    for j in range(chunks):
+                        col = j * slots + s
+                        spot = pl.multiple_of(j * lanes + at, SUB)
+                        x = jnp.broadcast_to(r_now[:, col : col + 1], (SUB, lanes))
+                        for n in range(chunks):
+                            part = tiles[s, pl.ds(spot, SUB), n * lanes : (n + 1) * lanes]
+                            accs[n * slots + s] = accs[n * slots + s] + part * x
+            return tuple(accs)
+
+        accs = lax.fori_loop(0, lanes // (SUB * UNROLL), transposed, (zero,) * (slots * chunks))
+        col_out[k] = select(put_col, jnp.concatenate(accs, axis=0))
+        sums = jnp.zeros((2, lanes), jnp.float32)
+        for d in range(nc):
+            sums = sums + row_in[k, d, COMP:SUB, :]
+        for d in range(nf):
+            col_out[k, d * slab + COMP : d * slab + SUB, :] = sums
+        backs = []
+        for d in range(1, nf):
+            peer = col_peers[d - 1]
+            part = col_out.at[k, pl.ds(pl.multiple_of(peer[0] * slab, SUB), slab), :]
+            backs.append(remote(part, col_back.at[k, f], s_colb.at[k, d], r_colb.at[k, d], peer))
+        col_back[k, f] = col_out[k, pl.ds(pl.multiple_of(f * slab, SUB), slab), :]
 
         halo.wait_recv()
         ext = v + [halo_in[k]]
         forward = [[zero] * COMP for _ in range(blocks)]
-        for o in range(1, reach_len + 1):
-            turned = [pltpu.roll(part, lanes - o, 1) for part in ext]
+        for b in range(COMP):
+            turned = [
+                pltpu.roll(jnp.broadcast_to(part[b : b + 1, :], (SUB, lanes)), lanes - SUB, 1, stride=1, stride_axis=0)
+                for part in ext
+            ]
             for h in range(blocks):
-                moved = jnp.where(lane_iota < lanes - o, turned[h], turned[h + 1])
+                moved = jnp.where(lane_iota - row_iota < lanes - SUB, turned[h], turned[h + 1])
                 for a in range(COMP):
-                    forward[h][a] = forward[h][a] + band[o - 1, a, h] * moved
+                    forward[h][a] = forward[h][a] + flipped[a, b, h] * moved
         quad = jnp.zeros((1, lanes), jnp.float32)
         for h in range(blocks):
             ahead = zero
@@ -229,62 +319,41 @@
             quad = quad + jnp.sum(ahead * v[h], axis=0, keepdims=True)
             image[h] = image[h] + ahead
 
-        for copy in gathers:
+        for copy in col_gets:
             copy.wait_recv()
-        rows_all = row_in[k].reshape(nc * slab, lanes)
         cols_all = col_in[k].reshape(nf * slab, lanes)
-        r_cols[...] = jnp.dot(pick_row[...], rows_all, precision=HIGH, preferred_element_type=jnp.float32).T
-        c_rows[...] = jnp.dot(pick_col[...], cols_all, precision=HIGH, preferred_element_type=jnp.float32)
-
-        @pl.when(k == 0)
-        def _():
-            load.wait()
-
-        def strip(i, accs):
-            accs = list(accs)
-            at = pl.multiple_of(i * SUB, SUB)
-            r_now = r_cols[pl.ds(at, SUB), :]
-            g_now = zero
-            for s in range(slots):
-                for j in range(chunks):
-                    col = j * slots + s
-                    spot = pl.multiple_of(j * lanes + at, SUB)
-                    x = jnp.broadcast_to(r_now[:, col : col + 1], (SUB, lanes))
-                    dots = zero
-                    for n in range(chunks):
-                        part = tiles[s, pl.ds(spot, SUB), n * lanes : (n + 1) * lanes]
-                        here = n * slots + s
-                        dots = dots + part * c_rows[here : here + 1, :]
-                        accs[here] = accs[here] + part * x
-                    g_now = jnp.where(lane_iota == col, jnp.sum(dots, axis=1, keepdims=True), g_now)
-            g_cols[pl.ds(at, SUB), :] = g_now
-            return tuple(accs)
-
-        accs = lax.fori_loop(0, lanes // SUB, strip, (zero,) * (slots * chunks))
-        for q in range(slots * chunks):
-            col_acc[q * SUB : (q + 1) * SUB, :] = accs[q]
+        c_rows[...] = select(pick_col, cols_all)
+
+        def direct(i, carry):
+            for u in range(UNROLL):
+                at = pl.multiple_of(i * (SUB * UNROLL) + u * SUB, SUB)
+                g_now = zero
+                for s in range(slots):
+                    for j in range(chunks):
+                        spot = pl.multiple_of(j * lanes + at, SUB)
+                        dots = None
+                        for n in range(chunks):
+                            part = tiles[s, pl.ds(spot, SUB), n * lanes : (n + 1) * lanes]
+                            here = n * slots + s
+                            term = part * c_rows[here : here + 1, :]
+                            dots = term if dots is None else dots + term
+                        g_now = jnp.where(
+                            lane_iota == j * slots + s, jnp.sum(dots, axis=1, keepdims=True), g_now
+                        )
+                g_cols[pl.ds(at, SUB), :] = g_now
+            return carry
+
+        lax.fori_loop(0, lanes // (SUB * UNROLL), direct, 0)
         gains = g_cols[...]
         quad = 2.0 * (quad + jnp.sum(gains * r_cols[...], axis=0, keepdims=True))
-        row_out[k] = jnp.dot(put_row[...], gains.T, precision=HIGH, preferred_element_type=jnp.float32)
-        col_out[k] = jnp.dot(put_col[...], col_acc[...], precision=HIGH, preferred_element_type=jnp.float32)
-        sums = jnp.zeros((2, lanes), jnp.float32)
-        for d in range(nc):
-            sums = sums + row_in[k, d, COMP:SUB, :]
-        for d in range(nf):
-            col_out[k, d * slab + COMP : d * slab + SUB, :] = sums
+        row_out[k] = select(put_row, gains.T)
         for d in range(nc):
             spot = (d + 1) * slab - SUB + COMP
             row_out[k, spot : spot + 1, :] = quad
-        backs = []
-        for d in range(1, nf):
-            peer = col_peers[d - 1]
-            part = col_out.at[k, pl.ds(pl.multiple_of(peer[0] * slab, SUB), slab), :]
-            backs.append(remote(part, col_back.at[k, f], s_colb.at[k, d], r_colb.at[k, d], peer))
         for d in range(1, nc):
             peer = row_peers[d - 1]
             part = row_out.at[k, pl.ds(pl.multiple_of(peer[1] * slab, SUB), slab), :]
             backs.append(remote(part, row_back.at[k, c], s_rowb.at[k, d], r_rowb.at[k, d], peer))
-        col_back[k, f] = col_out[k, pl.ds(pl.multiple_of(f * slab, SUB), slab), :]
         row_back[k, c] = row_out[k, pl.ds(pl.multiple_of(c * slab, SUB), slab), :]
         spilled.wait_recv()
         image[0] = image[0] + spill_in[k]
@@ -297,7 +366,7 @@
             image[h] = image[h] + swap_pairs(part, side)
             ys[k + 1, h] = image[h]
             vecs[k + 1, h] = precondition(h, image[h])
-        for copy in gathers + [halo, spilled] + backs:
+        for copy in col_gets + row_gets + [halo, spilled] + backs:
             copy.wait_send()
         return carry
 
@@ -374,11 +443,19 @@
     padded = -(-slots * chunks // lanes) * lanes
     f32 = jnp.float32
     vmem = pl.BlockSpec(memory_space=pltpu.VMEM)
-    smem = pl.BlockSpec(memory_space=pltpu.SMEM)
     dma = pltpu.SemaphoreType.DMA
+    bf16 = jnp.bfloat16
     scratch = [
+        pltpu.VMEM(right_side.shape, f32),
+        pltpu.VMEM(diag_blocks.shape, f32),
+        pltpu.VMEM((COMP, COMP, reach_len, frames), f32),
+        pltpu.VMEM((1, frames), jnp.int32),
+        pltpu.SMEM(tile_rows.shape, jnp.int32),
+        pltpu.SMEM(tile_cols.shape, jnp.int32),
+        pltpu.SMEM(tile_count.shape, jnp.int32),
         pltpu.VMEM((slots, tile, tile), f32),
-        pltpu.VMEM((reach_len, COMP, blocks, SUB, lanes), f32),
+        pltpu.VMEM((COMP, COMP, blocks, SUB, lanes), f32),
+        pltpu.VMEM((COMP, COMP, blocks, SUB, lanes), f32),
         pltpu.VMEM((COMP, blocks, SUB, lanes), f32),
         pltpu.VMEM((ITERS + 1, blocks, SUB, lanes), f32),
         pltpu.VMEM((ITERS + 1, blocks, SUB, lanes), f32),
@@ -393,32 +470,32 @@
         pltpu.VMEM((ITERS, nf, slab, lanes), f32),
         pltpu.VMEM((SUB, lanes), f32),
         pltpu.VMEM((nf, SUB, lanes), f32),
-        pltpu.VMEM((padded, nc * slab), f32),
-        pltpu.VMEM((padded, nf * slab), f32),
-        pltpu.VMEM((nc * slab, padded), f32),
-        pltpu.VMEM((nf * slab, slots * chunks * SUB), f32),
+        pltpu.VMEM((padded, 3 * nc * slab), bf16),
+        pltpu.VMEM((padded, 3 * nf * slab), bf16),
+        pltpu.VMEM((nc * slab, 3 * padded), bf16),
+        pltpu.VMEM((nf * slab, 3 * slots * chunks * SUB), bf16),
         pltpu.VMEM((lanes, padded), f32),
         pltpu.VMEM((padded, lanes), f32),
         pltpu.VMEM((lanes, padded), f32),
-        pltpu.VMEM((slots * chunks * SUB, lanes), f32),
         pltpu.VMEM((ITERS, slab, lanes), f32),
         dma,
+        dma((7,)),
     ]
     for shape in ((ITERS, nc), (ITERS, nf), (ITERS,), (ITERS,), (ITERS, nc), (ITERS, nf), (nf,)):
         scratch += [dma(shape), dma(shape)]
     return pl.pallas_call(
         functools.partial(kernel, nf, nc),
         out_shape=(jax.ShapeDtypeStruct(right_side.shape, f32), jax.ShapeDtypeStruct(right_side.shape, f32)),
-        in_specs=[vmem, vmem, vmem, vmem, pl.BlockSpec(memory_space=pl.ANY), smem, smem, smem],
+        in_specs=[pl.BlockSpec(memory_space=pltpu.HBM)] * 8,
         out_specs=(vmem, vmem),
         scratch_shapes=scratch,
         compiler_params=pltpu.CompilerParams(
-            collective_id=0, has_side_effects=True, vmem_limit_bytes=32 * 1024 * 1024
+            collective_id=0, has_side_effects=True, vmem_limit_bytes=60 * 1024 * 1024
         ),
         cost_estimate=pl.CostEstimate(
             flops=4 * ITERS * tiles.size, bytes_accessed=4 * (tiles.size + band_blocks.size), transcendentals=0
         ),
-    )(right_side, diag_blocks, band_blocks, reach.reshape(1, -1), tiles, tile_rows, tile_cols, tile_count)
+    )(right_side, diag_blocks, band_blocks.transpose(1, 2, 0, 3), reach.reshape(1, -1), tiles, tile_rows, tile_cols, tile_count)
 
 
 def solution(mesh):

time: 84.6 us -> 51.5 us (0.61)
  Pallas kernels: 74.9 us -> 47.3 us
  local copies, waits for them, and re-layouts: 8.08 us -> 2.59 us
    pallas_call x1, Pallas kernels: 74.9 us -> 47.3 us  [per_device(): pl.pallas_call(functools.partial(kernel, nf, nc), out_shape=(jax.ShapeDty...]
    unnamed x15 -> x2, local copies, waits for them, and re-layouts: 8.08 us -> 2.59 us
where the time goes in v2:
time: 51.5 us; the launch traced here: 51.2 us
  Pallas kernels  47.3 us (92%)
  local copies, waits for them, and re-layouts  2.59 us (5%)
  between operations  1.29 us (3%)
    pallas_call x1, Pallas kernels, per_device(): pl.pallas_call(functools.partial(kernel, nf, nc), out_shape=(jax.ShapeDty...  47.3 us
    unnamed x2, local copies, waits for them, and re-layouts  2.59 us

profile of v2, /device:TPU:0, one launch (start us, length us, event | category | flops | bytes accessed | tf_op | source)
XLA Modules:
  0.0 51.2 jit_solution(16033038600438807414)
XLA Ops:
  1.3 47.3 %shard_map.95 = (f32[6,256]{1,0:T(8,128)}, f32[6,256]{1,0:T(8,128)}) custom-call(f32[6,256]{1,0:T(8,128)} %rhs_hbm.1, f32[6,6,256]{2,1,0:T(8,128)} %diag_hbm.1, f32[6,6,8,256]{3,2,1,0:T(8,128)} %bitcast.2, s32[1,256]{1,0:T(1,128)} %bitcast.3, f32[1,1,8,384,384]{4,3,2,1,0:T(8,128)} %tiles_hbm.1, s32[1,1,8]{2,1,0:T(1,128)} %rows_hbm.1, s32[1,1,8]{2,1,0:T(1,128)} %cols_hbm.1, ...), custom_call_target="tpu_custom_call" | custom-call | flops 18874368 | bytes 5013504 | tf_op jit(solution)/shard_map/pallas_call | solution.py:486
  48.6 1.3 %copy.13 = f32[6,256]{1,0:T(8,128)} copy(f32[6,256]{1,0:T(8,128)} %get-tuple-element.4) | data formatting | bytes 12288
  49.9 1.3 %copy.14 = f32[6,256]{1,0:T(8,128)} copy(f32[6,256]{1,0:T(8,128)} %get-tuple-element.5) | data formatting | bytes 12288

commit v3 on v2

--- a/solution.py
+++ b/solution.py
@@ -44,8 +44,7 @@
     rows_hbm,
     cols_hbm,
     count_hbm,
-    sol_ref,
-    res_ref,
+    out_ref,
     rhs_ref,
     diag_ref,
     band_ref,
@@ -68,6 +67,8 @@
     col_out,
     row_back,
     col_back,
+    quad_out,
+    quad_in,
     last_out,
     last_in,
     pick_row,
@@ -77,6 +78,7 @@
     r_cols,
     c_rows,
     g_cols,
+    col_acc,
     nus,
     tile_sem,
     load_sem,
@@ -92,6 +94,8 @@
     r_rowb,
     s_colb,
     r_colb,
+    s_quad,
+    r_quad,
     s_last,
     r_last,
 ):
@@ -122,8 +126,9 @@
     ]
     for copy in small:
         copy.start()
-    load = pltpu.make_async_copy(tiles_hbm.at[0, 0], tiles, tile_sem)
-    load.start()
+    loads = [pltpu.make_async_copy(tiles_hbm.at[0, 0, t], tiles.at[t], tile_sem.at[t]) for t in range(slots)]
+    for copy in loads:
+        copy.start()
 
     row_peers = [(f, lax.rem(c + d, nc)) for d in range(1, nc)]
     col_peers = [(lax.rem(f + d, nf), c) for d in range(1, nf)]
@@ -140,7 +145,7 @@
 
     ys[0] = jnp.zeros((blocks, SUB, lanes), jnp.float32)
     inv[...] = jnp.zeros_like(inv)
-    for copy in small:
+    for copy in small[:2]:
         copy.wait()
     for h in range(blocks):
         cut = slice(h * lanes, (h + 1) * lanes)
@@ -171,6 +176,78 @@
     for h in range(blocks):
         vecs[0, h] = precondition(h, ys[0, h])
 
+    pl.semaphore_wait(barrier, len(greet))
+
+    def remote(src, dst, send, recv, peer):
+        return pltpu.make_async_remote_copy(
+            src_ref=src, dst_ref=dst, send_sem=send, recv_sem=recv, device_id=peer, device_id_type=MESH
+        )
+
+    def row_gathers(k):
+        return [
+            remote(row_in.at[k, c], row_in.at[k, c], s_row.at[k, d], r_row.at[k, d], row_peers[d - 1])
+            for d in range(1, nc)
+        ]
+
+    def col_gathers(k):
+        return [
+            remote(col_in.at[k, f], col_in.at[k, f], s_col.at[k, d], r_col.at[k, d], col_peers[d - 1])
+            for d in range(1, nf)
+        ]
+
+    def halo_copy(k):
+        return remote(vecs.at[k, 0], halo_in.at[k], s_halo.at[k], r_halo.at[k], before)
+
+    def spill_copy(k):
+        return remote(spill_out.at[k], spill_in.at[k], s_spill.at[k], r_spill.at[k], after)
+
+    def col_returns(k):
+        copies = []
+        for d in range(1, nf):
+            peer = col_peers[d - 1]
+            part = col_out.at[k, pl.ds(pl.multiple_of(peer[0] * slab, SUB), slab), :]
+            copies.append(remote(part, col_back.at[k, f], s_colb.at[k, d], r_colb.at[k, d], peer))
+        return copies
+
+    def row_returns(k):
+        copies = []
+        for d in range(1, nc):
+            peer = row_peers[d - 1]
+            part = row_out.at[k, pl.ds(pl.multiple_of(peer[1] * slab, SUB), slab), :]
+            copies.append(remote(part, row_back.at[k, c], s_rowb.at[k, d], r_rowb.at[k, d], peer))
+        return copies
+
+    def quad_copies():
+        return [remote(quad_out, quad_in.at[c], s_quad.at[d], r_quad.at[d], row_peers[d - 1]) for d in range(1, nc)]
+
+    def last_copies():
+        return [remote(last_out, last_in.at[f], s_last.at[d], r_last.at[d], col_peers[d - 1]) for d in range(1, nf)]
+
+    def sent(k):
+        for copy in row_gathers(k) + col_gathers(k) + [halo_copy(k), spill_copy(k)] + col_returns(k) + row_returns(k):
+            copy.wait_send()
+
+    def publish(k):
+        prev = jnp.maximum(k - 1, 0)
+        even = jnp.zeros((1, lanes), jnp.float32)
+        odd = jnp.zeros((1, lanes), jnp.float32)
+        for h in range(blocks):
+            y = ys[k, h]
+            even = even + jnp.sum(vecs[k, h] * y, axis=0, keepdims=True)
+            odd = odd + jnp.sum(vecs[prev, h] * y, axis=0, keepdims=True)
+        paired = [swap_pairs(vecs[k, h], side) for h in range(blocks)]
+        paired[0] = jnp.where(row_iota == COMP, even, jnp.where(row_iota == COMP + 1, odd, paired[0]))
+        for h in range(blocks):
+            row_in[k, c, h * SUB : (h + 1) * SUB, :] = paired[h]
+            col_in[k, f, h * SUB : (h + 1) * SUB, :] = paired[h]
+        for copy in row_gathers(k) + col_gathers(k) + [halo_copy(k)]:
+            copy.start()
+
+    publish(0)
+
+    for copy in small[2:]:
+        copy.wait()
+
     ends = (f == nf - 1) & (c == nc - 1)
     limit = jnp.where(ends, frames, frames + reach_len)
     for h in range(blocks):
@@ -206,15 +283,6 @@
         once = jnp.where(lax.broadcasted_iota(jnp.int32, (rows, wide), 0) == along, 1.0, 0.0)
         put[...] = jnp.concatenate([once] * 3, axis=1).astype(jnp.bfloat16)
 
-    pl.semaphore_wait(barrier, len(greet))
-
-    def remote(src, dst, send, recv, peer):
-        copy = pltpu.make_async_remote_copy(
-            src_ref=src, dst_ref=dst, send_sem=send, recv_sem=recv, device_id=peer, device_id_type=MESH
-        )
-        copy.start()
-        return copy
-
     def select(pick, value):
         first = value.astype(jnp.bfloat16)
         left = value - first.astype(jnp.float32)
@@ -224,25 +292,11 @@
         return jnp.dot(pick[...], parts, preferred_element_type=jnp.float32)
 
     def step(k, carry):
-        prev = jnp.maximum(k - 1, 0)
         v = [vecs[k, h] for h in range(blocks)]
-        even = jnp.zeros((1, lanes), jnp.float32)
-        odd = jnp.zeros((1, lanes), jnp.float32)
-        for h in range(blocks):
-            y = ys[k, h]
-            even = even + jnp.sum(v[h] * y, axis=0, keepdims=True)
-            odd = odd + jnp.sum(vecs[prev, h] * y, axis=0, keepdims=True)
-        paired = [swap_pairs(v[h], side) for h in range(blocks)]
-        paired[0] = jnp.where(row_iota == COMP, even, jnp.where(row_iota == COMP + 1, odd, paired[0]))
-        for h in range(blocks):
-            row_in[k, c, h * SUB : (h + 1) * SUB, :] = paired[h]
-            col_in[k, f, h * SUB : (h + 1) * SUB, :] = paired[h]
-        row_gets, col_gets = [], []
-        for d in range(1, nf):
-            col_gets.append(remote(col_in.at[k, f], col_in.at[k, f], s_col.at[k, d], r_col.at[k, d], col_peers[d - 1]))
-        for d in range(1, nc):
-            row_gets.append(remote(row_in.at[k, c], row_in.at[k, c], s_row.at[k, d], r_row.at[k, d], row_peers[d - 1]))
-        halo = remote(vecs.at[k, 0], halo_in.at[k], s_halo.at[k], r_halo.at[k], before)
+
+        @pl.when(k > 0)
+        def _():
+            sent(k - 1)
 
         image = [zero] * blocks
         spill = zero
@@ -259,16 +313,17 @@
             moved = jnp.sum(jnp.where(lane_iota > row_iota, 0.0, passed), axis=0, keepdims=True)
             spill = jnp.where(row_iota == b, moved, spill)
         spill_out[k] = spill
-        spilled = remote(spill_out.at[k], spill_in.at[k], s_spill.at[k], r_spill.at[k], after)
-
-        for copy in row_gets:
+        spill_copy(k).start()
+
+        for copy in row_gathers(k):
             copy.wait_recv()
         rows_all = row_in[k].reshape(nc * slab, lanes)
         r_cols[...] = select(pick_row, rows_all).T
 
         @pl.when(k == 0)
         def _():
-            load.wait()
+            for copy in loads:
+                copy.wait()
 
         def transposed(i, accs):
             accs = list(accs)
@@ -286,20 +341,19 @@
             return tuple(accs)
 
         accs = lax.fori_loop(0, lanes // (SUB * UNROLL), transposed, (zero,) * (slots * chunks))
-        col_out[k] = select(put_col, jnp.concatenate(accs, axis=0))
+        for q, acc in enumerate(accs):
+            col_acc[q * SUB : (q + 1) * SUB, :] = acc
+        col_out[k] = select(put_col, col_acc[...])
         sums = jnp.zeros((2, lanes), jnp.float32)
         for d in range(nc):
             sums = sums + row_in[k, d, COMP:SUB, :]
         for d in range(nf):
             col_out[k, d * slab + COMP : d * slab + SUB, :] = sums
-        backs = []
-        for d in range(1, nf):
-            peer = col_peers[d - 1]
-            part = col_out.at[k, pl.ds(pl.multiple_of(peer[0] * slab, SUB), slab), :]
-            backs.append(remote(part, col_back.at[k, f], s_colb.at[k, d], r_colb.at[k, d], peer))
+        for copy in col_returns(k):
+            copy.start()
         col_back[k, f] = col_out[k, pl.ds(pl.multiple_of(f * slab, SUB), slab), :]
 
-        halo.wait_recv()
+        halo_copy(k).wait_recv()
         ext = v + [halo_in[k]]
         forward = [[zero] * COMP for _ in range(blocks)]
         for b in range(COMP):
@@ -319,10 +373,21 @@
             quad = quad + jnp.sum(ahead * v[h], axis=0, keepdims=True)
             image[h] = image[h] + ahead
 
-        for copy in col_gets:
+        for copy in col_gathers(k):
             copy.wait_recv()
         cols_all = col_in[k].reshape(nf * slab, lanes)
         c_rows[...] = select(pick_col, cols_all)
+
+        @pl.when(k == last)
+        def _():
+            both = zero
+            for q in range(slots * chunks):
+                both = both + col_acc[q * SUB : (q + 1) * SUB, :] * c_rows[q : q + 1, :]
+            part = 2.0 * (quad + jnp.sum(both, axis=0, keepdims=True))
+            quad_out[...] = jnp.broadcast_to(part, (SUB, lanes))
+            for copy in quad_copies():
+                copy.start()
+            quad_in[c] = quad_out[...]
 
         def direct(i, carry):
             for u in range(UNROLL):
@@ -344,40 +409,41 @@
             return carry
 
         lax.fori_loop(0, lanes // (SUB * UNROLL), direct, 0)
-        gains = g_cols[...]
-        quad = 2.0 * (quad + jnp.sum(gains * r_cols[...], axis=0, keepdims=True))
-        row_out[k] = select(put_row, gains.T)
-        for d in range(nc):
-            spot = (d + 1) * slab - SUB + COMP
-            row_out[k, spot : spot + 1, :] = quad
-        for d in range(1, nc):
-            peer = row_peers[d - 1]
-            part = row_out.at[k, pl.ds(pl.multiple_of(peer[1] * slab, SUB), slab), :]
-            backs.append(remote(part, row_back.at[k, c], s_rowb.at[k, d], r_rowb.at[k, d], peer))
+
+        @pl.when(k == last)
+        def _():
+            for copy in quad_copies():
+                copy.wait_recv()
+            last_out[...] = jnp.sum(quad_in[...], axis=0)
+            for copy in last_copies():
+                copy.start()
+            last_in[f] = last_out[...]
+
+        row_out[k] = select(put_row, g_cols[...].T)
+        for copy in row_returns(k):
+            copy.start()
         row_back[k, c] = row_out[k, pl.ds(pl.multiple_of(c * slab, SUB), slab), :]
-        spilled.wait_recv()
+        spill_copy(k).wait_recv()
         image[0] = image[0] + spill_in[k]
-        for copy in backs:
+        for copy in col_returns(k) + row_returns(k):
             copy.wait_recv()
         total = jnp.sum(row_back[k], axis=0) + jnp.sum(col_back[k], axis=0)
-        nus[k] = total
+        nus[k] = total[0:SUB, :]
         for h in range(blocks):
             part = jnp.where(row_iota < COMP, total[h * SUB : (h + 1) * SUB, :], 0.0)
             image[h] = image[h] + swap_pairs(part, side)
             ys[k + 1, h] = image[h]
-            vecs[k + 1, h] = precondition(h, image[h])
-        for copy in col_gets + row_gets + [halo, spilled] + backs:
-            copy.wait_send()
+
+        @pl.when(k < last)
+        def _():
+            for h in range(blocks):
+                vecs[k + 1, h] = precondition(h, image[h])
+            publish(k + 1)
+
         return carry
 
+    last = ITERS - 1
     lax.fori_loop(0, ITERS, step, 0)
-
-    last = ITERS - 1
-    last_out[...] = nus[last, slab - SUB : slab, :]
-    finals = []
-    for d in range(1, nf):
-        finals.append(remote(last_out, last_in.at[f], s_last.at[d], r_last.at[d], col_peers[d - 1]))
-    last_in[f] = last_out[...]
 
     moments = []
     for k in range(ITERS):
@@ -404,9 +470,9 @@
     gamma = quadratic(rho, lambda at: moments[at])
     for iteration in range(ITERS):
         if iteration == last:
-            for copy in finals:
+            for copy in last_copies():
                 copy.wait_recv()
-            ending = jnp.sum(last_in[...], axis=0)[COMP : COMP + 1, :]
+            ending = jnp.sum(last_in[...], axis=0)[0:1, :]
             moments.append(jnp.sum(ending, axis=1, keepdims=True))
         alpha = gamma / quadratic(pi, lambda at: moments[at] + moments[at + 1])
         xi = [x + alpha * p for x, p in zip(xi + [none] * (len(pi) - len(xi)), pi)]
@@ -426,9 +492,10 @@
             sol = sol + xi[k] * vecs[k, h]
         for k in range(ITERS + 1):
             res = res + rho[k] * ys[k, h]
-        sol_ref[:, cut] = sol[0:COMP, :]
-        res_ref[:, cut] = res[0:COMP, :]
-    for copy in finals:
+        out_ref[0, :, cut] = sol[0:COMP, :]
+        out_ref[1, :, cut] = res[0:COMP, :]
+    sent(last)
+    for copy in quad_copies() + last_copies():
         copy.wait_send()
 
 
@@ -469,6 +536,8 @@
         pltpu.VMEM((ITERS, nc, slab, lanes), f32),
         pltpu.VMEM((ITERS, nf, slab, lanes), f32),
         pltpu.VMEM((SUB, lanes), f32),
+        pltpu.VMEM((nc, SUB, lanes), f32),
+        pltpu.VMEM((SUB, lanes), f32),
         pltpu.VMEM((nf, SUB, lanes), f32),
         pltpu.VMEM((padded, 3 * nc * slab), bf16),
         pltpu.VMEM((padded, 3 * nf * slab), bf16),
@@ -477,17 +546,18 @@
         pltpu.VMEM((lanes, padded), f32),
         pltpu.VMEM((padded, lanes), f32),
         pltpu.VMEM((lanes, padded), f32),
-        pltpu.VMEM((ITERS, slab, lanes), f32),
-        dma,
+        pltpu.VMEM((slots * chunks * SUB, lanes), f32),
+        pltpu.VMEM((ITERS, SUB, lanes), f32),
+        dma((slots,)),
         dma((7,)),
     ]
-    for shape in ((ITERS, nc), (ITERS, nf), (ITERS,), (ITERS,), (ITERS, nc), (ITERS, nf), (nf,)):
+    for shape in ((ITERS, nc), (ITERS, nf), (ITERS,), (ITERS,), (ITERS, nc), (ITERS, nf), (nc,), (nf,)):
         scratch += [dma(shape), dma(shape)]
-    return pl.pallas_call(
+    out = pl.pallas_call(
         functools.partial(kernel, nf, nc),
-        out_shape=(jax.ShapeDtypeStruct(right_side.shape, f32), jax.ShapeDtypeStruct(right_side.shape, f32)),
+        out_shape=jax.ShapeDtypeStruct((2,) + right_side.shape, f32),
         in_specs=[pl.BlockSpec(memory_space=pltpu.HBM)] * 8,
-        out_specs=(vmem, vmem),
+        out_specs=vmem,
         scratch_shapes=scratch,
         compiler_params=pltpu.CompilerParams(
             collective_id=0, has_side_effects=True, vmem_limit_bytes=60 * 1024 * 1024
@@ -496,6 +566,7 @@
             flops=4 * ITERS * tiles.size, bytes_accessed=4 * (tiles.size + band_blocks.size), transcendentals=0
         ),
     )(right_side, diag_blocks, band_blocks.transpose(1, 2, 0, 3), reach.reshape(1, -1), tiles, tile_rows, tile_cols, tile_count)
+    return out[0], out[1]
 
 
 def solution(mesh):

time: 51.5 us -> 49 us (0.951)
  local copies, waits for them, and re-layouts: 2.59 us -> 1.32 us
  Pallas kernels: 47.3 us -> 46.2 us
    unnamed x2 -> x0, local copies, waits for them, and re-layouts: 2.59 us -> none
    squeeze x0 -> x1, local copies, waits for them, and re-layouts: none -> 1.32 us  [per_device(): return (out[0], out[1])]
    pallas_call x1, Pallas kernels: 47.3 us -> 46.2 us  [per_device(): pl.pallas_call(functools.partial(kernel, nf, nc), out_shape=jax.ShapeDtyp...]
where the time goes in v3:
time: 49 us; the launch traced here: 48.8 us
  Pallas kernels  46.2 us (94%)
  local copies, waits for them, and re-layouts  1.32 us (3%)
  between operations  1.29 us (3%)
    pallas_call x1, Pallas kernels, per_device(): pl.pallas_call(functools.partial(kernel, nf, nc), out_shape=jax.ShapeDtyp...  46.2 us
    squeeze x1, local copies, waits for them, and re-layouts, per_device(): return (out[0], out[1])  1.32 us

profile of v3, /device:TPU:0, one launch (start us, length us, event | category | flops | bytes accessed | tf_op | source)
XLA Modules:
  0.0 48.8 jit_solution(8410980746520284209)
XLA Ops:
  1.3 46.2 %shard_map.95 = f32[2,6,256]{2,1,0:T(8,128)} custom-call(f32[6,256]{1,0:T(8,128)} %rhs_hbm.1, f32[6,6,256]{2,1,0:T(8,128)} %diag_hbm.1, f32[6,6,8,256]{3,2,1,0:T(8,128)} %bitcast.6, s32[1,256]{1,0:T(1,128)} %bitcast.7, f32[1,1,8,384,384]{4,3,2,1,0:T(8,128)} %tiles_hbm.1, s32[1,1,8]{2,1,0:T(1,128)} %rows_hbm.1, s32[1,1,8]{2,1,0:T(1,128)} %cols_hbm.1, ...), custom_call_target="tpu_custom_call" | custom-call | flops 18874368 | bytes 5013504 | tf_op jit(solution)/shard_map/pallas_call | solution.py:556
  47.5 1.3 %slice_bitcast_fusion = (f32[6,256]{1,0:T(8,128)}, f32[6,256]{1,0:T(8,128)}) fusion(f32[2,6,256]{2,1,0:T(8,128)} %shard_map.95), kind=kLoop, calls=%fused_computation | loop fusion | bytes 24576 | tf_op jit(solution)/shard_map/squeeze | solution.py:569

commit v4 on v3

--- a/solution.py
+++ b/solution.py
@@ -10,7 +10,7 @@
 ITERS = 4
 COMP = 6
 SUB = 8
-UNROLL = 4
+PART = 32
 MESH = pl.DeviceIdType.MESH
 
 
@@ -53,6 +53,8 @@
     cols_ref,
     count_ref,
     tiles,
+    high,
+    low,
     band,
     flipped,
     inv,
@@ -75,9 +77,6 @@
     pick_col,
     put_row,
     put_col,
-    r_cols,
-    c_rows,
-    g_cols,
     col_acc,
     nus,
     tile_sem,
@@ -263,23 +262,22 @@
 
     count = count_ref[0, 0]
 
-    def targets(ids_ref, iota, width):
+    def targets(ids_ref, iota):
         out = jnp.full(iota.shape, -1, jnp.int32)
-        slot_at = iota // width
         for s in range(slots):
             at = ids_ref[0, 0, s]
             base = jnp.where(s < count, (at // 2) * SUB + lax.rem(at, 2), -slab * nf * nc)
             for j in range(chunks):
-                out = jnp.where(slot_at == j * slots + s, base + 2 * j, out)
+                out = jnp.where(iota == j * slots + s, base + 2 * j, out)
         return out
 
-    for ids, pick, put, width in ((rows_ref, pick_row, put_row, 1), (cols_ref, pick_col, put_col, SUB)):
+    for ids, pick, put in ((rows_ref, pick_row, put_row), (cols_ref, pick_col, put_col)):
         rows, wide = pick.shape[0], pick.shape[1] // 3
-        down = targets(ids, lax.broadcasted_iota(jnp.int32, (rows, 1), 0), 1)
+        down = targets(ids, lax.broadcasted_iota(jnp.int32, (rows, 1), 0))
         once = jnp.where(lax.broadcasted_iota(jnp.int32, (rows, wide), 1) == down, 1.0, 0.0)
         pick[...] = jnp.concatenate([once] * 3, axis=1).astype(jnp.bfloat16)
         rows, wide = put.shape[0], put.shape[1] // 3
-        along = targets(ids, lax.broadcasted_iota(jnp.int32, (1, wide), 1), width)
+        along = targets(ids, lax.broadcasted_iota(jnp.int32, (1, wide), 1))
         once = jnp.where(lax.broadcasted_iota(jnp.int32, (rows, wide), 0) == along, 1.0, 0.0)
         put[...] = jnp.concatenate([once] * 3, axis=1).astype(jnp.bfloat16)
 
@@ -290,6 +288,43 @@
         third = (left - second.astype(jnp.float32)).astype(jnp.bfloat16)
         parts = jnp.concatenate([first, second, third], axis=0)
         return jnp.dot(pick[...], parts, preferred_element_type=jnp.float32)
+
+    tile_row = lax.broadcasted_iota(jnp.int32, (slots, tile), 0)
+    many = slots * chunks
+
+    def products(rows, contract):
+        value = jnp.concatenate([rows[j * slots : (j + 1) * slots, :] for j in range(chunks)], axis=1)
+        first = value.astype(jnp.bfloat16).astype(jnp.float32)
+        second = (value - first).astype(jnp.bfloat16).astype(jnp.float32)
+        third = value - first - second
+        left = jnp.concatenate([first, second, third, jnp.zeros_like(third)], axis=0).astype(jnp.bfloat16)
+        out = jnp.zeros((slots, tile), jnp.float32)
+        for s in range(slots):
+            full = None
+            for part in (high, low):
+                term = lax.dot_general(
+                    left, part[s], (((1,), (contract,)), ((), ())), preferred_element_type=jnp.float32
+                )
+                full = term if full is None else full + term
+            kept = full[:slots] + full[slots : 2 * slots] + full[2 * slots : 3 * slots]
+            out = jnp.where(tile_row == s, kept, out)
+        pieces = [out[:, j * lanes : (j + 1) * lanes] for j in range(chunks)]
+        if rows.shape[0] > many:
+            pieces.append(jnp.zeros((rows.shape[0] - many, lanes), jnp.float32))
+        return jnp.concatenate(pieces, axis=0)
+
+    for s in range(slots):
+        loads[s].wait()
+
+        def split(i, carry, s=s):
+            spot = pl.ds(pl.multiple_of(i * PART, PART), PART)
+            whole = tiles[s, spot, :]
+            first = whole.astype(jnp.bfloat16)
+            high[s, spot, :] = first
+            low[s, spot, :] = (whole - first.astype(jnp.float32)).astype(jnp.bfloat16)
+            return carry
+
+        lax.fori_loop(0, tile // PART, split, 0)
 
     def step(k, carry):
         v = [vecs[k, h] for h in range(blocks)]
@@ -317,32 +352,7 @@
 
         for copy in row_gathers(k):
             copy.wait_recv()
-        rows_all = row_in[k].reshape(nc * slab, lanes)
-        r_cols[...] = select(pick_row, rows_all).T
-
-        @pl.when(k == 0)
-        def _():
-            for copy in loads:
-                copy.wait()
-
-        def transposed(i, accs):
-            accs = list(accs)
-            for u in range(UNROLL):
-                at = pl.multiple_of(i * (SUB * UNROLL) + u * SUB, SUB)
-                r_now = r_cols[pl.ds(at, SUB), :]
-                for s in range(slots):
-                    for j in range(chunks):
-                        col = j * slots + s
-                        spot = pl.multiple_of(j * lanes + at, SUB)
-                        x = jnp.broadcast_to(r_now[:, col : col + 1], (SUB, lanes))
-                        for n in range(chunks):
-                            part = tiles[s, pl.ds(spot, SUB), n * lanes : (n + 1) * lanes]
-                            accs[n * slots + s] = accs[n * slots + s] + part * x
-            return tuple(accs)
-
-        accs = lax.fori_loop(0, lanes // (SUB * UNROLL), transposed, (zero,) * (slots * chunks))
-        for q, acc in enumerate(accs):
-            col_acc[q * SUB : (q + 1) * SUB, :] = acc
+        col_acc[...] = products(select(pick_row, row_in[k].reshape(nc * slab, lanes)), 0)
         col_out[k] = select(put_col, col_acc[...])
         sums = jnp.zeros((2, lanes), jnp.float32)
         for d in range(nc):
@@ -375,40 +385,17 @@
 
         for copy in col_gathers(k):
             copy.wait_recv()
-        cols_all = col_in[k].reshape(nf * slab, lanes)
-        c_rows[...] = select(pick_col, cols_all)
+        c_rows = select(pick_col, col_in[k].reshape(nf * slab, lanes))
 
         @pl.when(k == last)
         def _():
-            both = zero
-            for q in range(slots * chunks):
-                both = both + col_acc[q * SUB : (q + 1) * SUB, :] * c_rows[q : q + 1, :]
-            part = 2.0 * (quad + jnp.sum(both, axis=0, keepdims=True))
+            part = 2.0 * (quad + jnp.sum(col_acc[...] * c_rows, axis=0, keepdims=True))
             quad_out[...] = jnp.broadcast_to(part, (SUB, lanes))
             for copy in quad_copies():
                 copy.start()
             quad_in[c] = quad_out[...]
 
-        def direct(i, carry):
-            for u in range(UNROLL):
-                at = pl.multiple_of(i * (SUB * UNROLL) + u * SUB, SUB)
-                g_now = zero
-                for s in range(slots):
-                    for j in range(chunks):
-                        spot = pl.multiple_of(j * lanes + at, SUB)
-                        dots = None
-                        for n in range(chunks):
-                            part = tiles[s, pl.ds(spot, SUB), n * lanes : (n + 1) * lanes]
-                            here = n * slots + s
-                            term = part * c_rows[here : here + 1, :]
-                            dots = term if dots is None else dots + term
-                        g_now = jnp.where(
-                            lane_iota == j * slots + s, jnp.sum(dots, axis=1, keepdims=True), g_now
-                        )
-                g_cols[pl.ds(at, SUB), :] = g_now
-            return carry
-
-        lax.fori_loop(0, lanes // (SUB * UNROLL), direct, 0)
+        gains = products(c_rows, 1)
 
         @pl.when(k == last)
         def _():
@@ -419,7 +406,7 @@
                 copy.start()
             last_in[f] = last_out[...]
 
-        row_out[k] = select(put_row, g_cols[...].T)
+        row_out[k] = select(put_row, gains)
         for copy in row_returns(k):
             copy.start()
         row_back[k, c] = row_out[k, pl.ds(pl.multiple_of(c * slab, SUB), slab), :]
@@ -507,7 +494,7 @@
     blocks = frames // lanes
     slab = blocks * SUB
     reach_len = band_blocks.shape[0]
-    padded = -(-slots * chunks // lanes) * lanes
+    padded = -(-slots * chunks // (2 * SUB)) * 2 * SUB
     f32 = jnp.float32
     vmem = pl.BlockSpec(memory_space=pltpu.VMEM)
     dma = pltpu.SemaphoreType.DMA
@@ -521,6 +508,8 @@
         pltpu.SMEM(tile_cols.shape, jnp.int32),
         pltpu.SMEM(tile_count.shape, jnp.int32),
         pltpu.VMEM((slots, tile, tile), f32),
+        pltpu.VMEM((slots, tile, tile), bf16),
+        pltpu.VMEM((slots, tile, tile), bf16),
         pltpu.VMEM((COMP, COMP, blocks, SUB, lanes), f32),
         pltpu.VMEM((COMP, COMP, blocks, SUB, lanes), f32),
         pltpu.VMEM((COMP, blocks, SUB, lanes), f32),
@@ -542,11 +531,8 @@
         pltpu.VMEM((padded, 3 * nc * slab), bf16),
         pltpu.VMEM((padded, 3 * nf * slab), bf16),
         pltpu.VMEM((nc * slab, 3 * padded), bf16),
-        pltpu.VMEM((nf * slab, 3 * slots * chunks * SUB), bf16),
-        pltpu.VMEM((lanes, padded), f32),
+        pltpu.VMEM((nf * slab, 3 * padded), bf16),
         pltpu.VMEM((padded, lanes), f32),
-        pltpu.VMEM((lanes, padded), f32),
-        pltpu.VMEM((slots * chunks * SUB, lanes), f32),
         pltpu.VMEM((ITERS, SUB, lanes), f32),
         dma((slots,)),
         dma((7,)),

time: 49 us -> 50 us (1.020)
  Pallas kernels: 46.2 us -> 47.2 us
    pallas_call x1, Pallas kernels: 46.2 us -> 47.2 us  [per_device(): pl.pallas_call(functools.partial(kernel, nf, nc), out_shape=jax.ShapeDtyp...]
where the time goes in v4:
time: 50 us; the launch traced here: 49.8 us
  Pallas kernels  47.2 us (94%)
  local copies, waits for them, and re-layouts  1.32 us (3%)
  between operations  1.29 us (3%)
    pallas_call x1, Pallas kernels, per_device(): pl.pallas_call(functools.partial(kernel, nf, nc), out_shape=jax.ShapeDtyp...  47.2 us
    squeeze x1, local copies, waits for them, and re-layouts, per_device(): return (out[0], out[1])  1.32 us

profile of v4, /device:TPU:0, one launch (start us, length us, event | category | flops | bytes accessed | tf_op | source)
XLA Modules:
  0.0 49.8 jit_solution(17448150575261987350)
XLA Ops:
  1.3 47.2 %shard_map.95 = f32[2,6,256]{2,1,0:T(8,128)} custom-call(f32[6,256]{1,0:T(8,128)} %rhs_hbm.1, f32[6,6,256]{2,1,0:T(8,128)} %diag_hbm.1, f32[6,6,8,256]{3,2,1,0:T(8,128)} %bitcast.6, s32[1,256]{1,0:T(1,128)} %bitcast.7, f32[1,1,8,384,384]{4,3,2,1,0:T(8,128)} %tiles_hbm.1, s32[1,1,8]{2,1,0:T(1,128)} %rows_hbm.1, s32[1,1,8]{2,1,0:T(1,128)} %cols_hbm.1, ...), custom_call_target="tpu_custom_call" | custom-call | flops 18874368 | bytes 5013504 | tf_op jit(solution)/shard_map/pallas_call | solution.py:542
  48.5 1.3 %slice_bitcast_fusion = (f32[6,256]{1,0:T(8,128)}, f32[6,256]{1,0:T(8,128)}) fusion(f32[2,6,256]{2,1,0:T(8,128)} %shard_map.95), kind=kLoop, calls=%fused_computation | loop fusion | bytes 24576 | tf_op jit(solution)/shard_map/squeeze | solution.py:555

commit v5 on v3

--- a/solution.py
+++ b/solution.py
@@ -134,10 +134,31 @@
     col_peers = [(lax.rem(f + d, nf), c) for d in range(1, nf)]
     after = (lax.rem(f + (c + 1) // nc, nf), lax.rem(c + 1, nc))
     before = (lax.rem(f + nf - 1 + (c + nc - 1) // nc, nf), lax.rem(c + nc - 1, nc))
-    greet = row_peers + col_peers + [after, before]
+    is_first = (f == 0) & (c == 0)
+    is_last = (f == nf - 1) & (c == nc - 1)
     barrier = pltpu.get_barrier_semaphore()
-    for peer in greet:
+
+    def greet(peer):
         pl.semaphore_signal(barrier, inc=1, device_id=peer, device_id_type=MESH)
+
+    for peer in col_peers + row_peers:
+        greet(peer)
+
+    @pl.when(jnp.logical_not(is_first))
+    def _():
+        greet(before)
+
+    @pl.when(jnp.logical_not(is_last))
+    def _():
+        greet(after)
+
+    @pl.when(is_first)
+    def _():
+        spill_in[...] = jnp.zeros_like(spill_in)
+
+    @pl.when(is_last)
+    def _():
+        halo_in[...] = jnp.zeros_like(halo_in)
 
     row_iota = lax.broadcasted_iota(jnp.int32, (SUB, lanes), 0)
     lane_iota = lax.broadcasted_iota(jnp.int32, (SUB, lanes), 1)
@@ -176,7 +197,13 @@
     for h in range(blocks):
         vecs[0, h] = precondition(h, ys[0, h])
 
-    pl.semaphore_wait(barrier, len(greet))
+    ends = jnp.where(is_first, 1, 0) + jnp.where(is_last, 1, 0)
+    pl.semaphore_wait(barrier, len(col_peers) + len(row_peers) + 2 - ends)
+
+    def unless(edge, act):
+        @pl.when(jnp.logical_not(edge))
+        def _():
+            act()
 
     def remote(src, dst, send, recv, peer):
         return pltpu.make_async_remote_copy(
@@ -224,8 +251,10 @@
         return [remote(last_out, last_in.at[f], s_last.at[d], r_last.at[d], col_peers[d - 1]) for d in range(1, nf)]
 
     def sent(k):
-        for copy in row_gathers(k) + col_gathers(k) + [halo_copy(k), spill_copy(k)] + col_returns(k) + row_returns(k):
+        for copy in row_gathers(k) + col_gathers(k) + col_returns(k) + row_returns(k):
             copy.wait_send()
+        unless(is_first, lambda: halo_copy(k).wait_send())
+        unless(is_last, lambda: spill_copy(k).wait_send())
 
     def publish(k):
         prev = jnp.maximum(k - 1, 0)
@@ -240,16 +269,16 @@
         for h in range(blocks):
             row_in[k, c, h * SUB : (h + 1) * SUB, :] = paired[h]
             col_in[k, f, h * SUB : (h + 1) * SUB, :] = paired[h]
-        for copy in row_gathers(k) + col_gathers(k) + [halo_copy(k)]:
+        for copy in row_gathers(k) + col_gathers(k):
             copy.start()
+        unless(is_first, lambda: halo_copy(k).start())
 
     publish(0)
 
     for copy in small[2:]:
         copy.wait()
 
-    ends = (f == nf - 1) & (c == nc - 1)
-    limit = jnp.where(ends, frames, frames + reach_len)
+    limit = jnp.where(is_last, frames, frames + reach_len)
     for h in range(blocks):
         cut = slice(h * lanes, (h + 1) * lanes)
         offset = row_iota + 1
@@ -313,7 +342,7 @@
             moved = jnp.sum(jnp.where(lane_iota > row_iota, 0.0, passed), axis=0, keepdims=True)
             spill = jnp.where(row_iota == b, moved, spill)
         spill_out[k] = spill
-        spill_copy(k).start()
+        unless(is_last, lambda: spill_copy(k).start())
 
         for copy in row_gathers(k):
             copy.wait_recv()
@@ -353,7 +382,7 @@
             copy.start()
         col_back[k, f] = col_out[k, pl.ds(pl.multiple_of(f * slab, SUB), slab), :]
 
-        halo_copy(k).wait_recv()
+        unless(is_last, lambda: halo_copy(k).wait_recv())
         ext = v + [halo_in[k]]
         forward = [[zero] * COMP for _ in range(blocks)]
         for b in range(COMP):
@@ -423,7 +452,7 @@
         for copy in row_returns(k):
             copy.start()
         row_back[k, c] = row_out[k, pl.ds(pl.multiple_of(c * slab, SUB), slab), :]
-        spill_copy(k).wait_recv()
+        unless(is_first, lambda: spill_copy(k).wait_recv())
         image[0] = image[0] + spill_in[k]
         for copy in col_returns(k) + row_returns(k):
             copy.wait_recv()

time: 49 us -> 49 us (level)
  no operation moved by 1% of the time
where the time goes in v5:
time: 49 us; the launch traced here: 48.8 us
  Pallas kernels  46.2 us (94%)
  local copies, waits for them, and re-layouts  1.32 us (3%)
  between operations  1.29 us (3%)
    pallas_call x1, Pallas kernels, per_device(): pl.pallas_call(functools.partial(kernel, nf, nc), out_shape=jax.ShapeDtyp...  46.2 us
    squeeze x1, local copies, waits for them, and re-layouts, per_device(): return (out[0], out[1])  1.32 us

profile of v5, /device:TPU:0, one launch (start us, length us, event | category | flops | bytes accessed | tf_op | source)
XLA Modules:
  0.0 48.8 jit_solution(16005547791568686304)
XLA Ops:
  1.3 46.2 %shard_map.95 = f32[2,6,256]{2,1,0:T(8,128)} custom-call(f32[6,256]{1,0:T(8,128)} %rhs_hbm.1, f32[6,6,256]{2,1,0:T(8,128)} %diag_hbm.1, f32[6,6,8,256]{3,2,1,0:T(8,128)} %bitcast.6, s32[1,256]{1,0:T(1,128)} %bitcast.7, f32[1,1,8,384,384]{4,3,2,1,0:T(8,128)} %tiles_hbm.1, s32[1,1,8]{2,1,0:T(1,128)} %rows_hbm.1, s32[1,1,8]{2,1,0:T(1,128)} %cols_hbm.1, ...), custom_call_target="tpu_custom_call" | custom-call | flops 18874368 | bytes 5013504 | tf_op jit(solution)/shard_map/pallas_call | solution.py:585
  47.5 1.3 %slice_bitcast_fusion = (f32[6,256]{1,0:T(8,128)}, f32[6,256]{1,0:T(8,128)}) fusion(f32[2,6,256]{2,1,0:T(8,128)} %shard_map.95), kind=kLoop, calls=%fused_computation | loop fusion | bytes 24576 | tf_op jit(solution)/shard_map/squeeze | solution.py:598

commit v6 on v5

--- a/solution.py
+++ b/solution.py
@@ -292,33 +292,32 @@
 
     count = count_ref[0, 0]
 
-    def targets(ids_ref, iota, width):
+    def targets(ids_ref, iota):
         out = jnp.full(iota.shape, -1, jnp.int32)
-        slot_at = iota // width
         for s in range(slots):
             at = ids_ref[0, 0, s]
             base = jnp.where(s < count, (at // 2) * SUB + lax.rem(at, 2), -slab * nf * nc)
             for j in range(chunks):
-                out = jnp.where(slot_at == j * slots + s, base + 2 * j, out)
+                out = jnp.where(iota == j * slots + s, base + 2 * j, out)
         return out
 
-    for ids, pick, put, width in ((rows_ref, pick_row, put_row, 1), (cols_ref, pick_col, put_col, SUB)):
-        rows, wide = pick.shape[0], pick.shape[1] // 3
-        down = targets(ids, lax.broadcasted_iota(jnp.int32, (rows, 1), 0), 1)
+    for ids, pick, put in ((rows_ref, pick_row, put_row), (cols_ref, pick_col, put_col)):
+        rows, wide = pick.shape[0], pick.shape[1] // 2
+        down = targets(ids, lax.broadcasted_iota(jnp.int32, (rows, 1), 0))
         once = jnp.where(lax.broadcasted_iota(jnp.int32, (rows, wide), 1) == down, 1.0, 0.0)
-        pick[...] = jnp.concatenate([once] * 3, axis=1).astype(jnp.bfloat16)
-        rows, wide = put.shape[0], put.shape[1] // 3
-        along = targets(ids, lax.broadcasted_iota(jnp.int32, (1, wide), 1), width)
+        pick[...] = jnp.concatenate([once] * 2, axis=1).astype(jnp.bfloat16)
+        rows, wide = put.shape[0], put.shape[1] // 2
+        along = targets(ids, lax.broadcasted_iota(jnp.int32, (1, wide), 1))
         once = jnp.where(lax.broadcasted_iota(jnp.int32, (rows, wide), 0) == along, 1.0, 0.0)
-        put[...] = jnp.concatenate([once] * 3, axis=1).astype(jnp.bfloat16)
+        put[...] = jnp.concatenate([once] * 2, axis=1).astype(jnp.bfloat16)
 
     def select(pick, value):
         first = value.astype(jnp.bfloat16)
-        left = value - first.astype(jnp.float32)
-        second = left.astype(jnp.bfloat16)
-        third = (left - second.astype(jnp.float32)).astype(jnp.bfloat16)
-        parts = jnp.concatenate([first, second, third], axis=0)
+        second = (value - first.astype(jnp.float32)).astype(jnp.bfloat16)
+        parts = jnp.concatenate([first, second], axis=0)
         return jnp.dot(pick[...], parts, preferred_element_type=jnp.float32)
+
+    slot_row = lax.broadcasted_iota(jnp.int32, (slots, lanes), 0)
 
     def step(k, carry):
         v = [vecs[k, h] for h in range(blocks)]
@@ -356,22 +355,27 @@
 
         def transposed(i, accs):
             accs = list(accs)
-            for u in range(UNROLL):
-                at = pl.multiple_of(i * (SUB * UNROLL) + u * SUB, SUB)
-                r_now = r_cols[pl.ds(at, SUB), :]
-                for s in range(slots):
+            at = [pl.multiple_of((i * UNROLL + u) * SUB, SUB) for u in range(UNROLL)]
+            r_now = [r_cols[pl.ds(at[u], SUB), :] for u in range(UNROLL)]
+            for s in range(slots):
+                for u in range(UNROLL):
                     for j in range(chunks):
                         col = j * slots + s
-                        spot = pl.multiple_of(j * lanes + at, SUB)
-                        x = jnp.broadcast_to(r_now[:, col : col + 1], (SUB, lanes))
+                        spot = pl.multiple_of(j * lanes + at[u], SUB)
+                        x = jnp.broadcast_to(r_now[u][:, col : col + 1], (SUB, lanes))
                         for n in range(chunks):
                             part = tiles[s, pl.ds(spot, SUB), n * lanes : (n + 1) * lanes]
                             accs[n * slots + s] = accs[n * slots + s] + part * x
             return tuple(accs)
 
         accs = lax.fori_loop(0, lanes // (SUB * UNROLL), transposed, (zero,) * (slots * chunks))
-        for q, acc in enumerate(accs):
-            col_acc[q * SUB : (q + 1) * SUB, :] = acc
+        col_acc[...] = jnp.zeros_like(col_acc)
+        for n in range(chunks):
+            folded = jnp.zeros((slots, lanes), jnp.float32)
+            for s in range(slots):
+                summed = jnp.sum(accs[n * slots + s], axis=0, keepdims=True)
+                folded = jnp.where(slot_row == s, summed, folded)
+            col_acc[n * slots : (n + 1) * slots, :] = folded
         col_out[k] = select(put_col, col_acc[...])
         sums = jnp.zeros((2, lanes), jnp.float32)
         for d in range(nc):
@@ -409,32 +413,30 @@
 
         @pl.when(k == last)
         def _():
-            both = zero
-            for q in range(slots * chunks):
-                both = both + col_acc[q * SUB : (q + 1) * SUB, :] * c_rows[q : q + 1, :]
-            part = 2.0 * (quad + jnp.sum(both, axis=0, keepdims=True))
+            part = 2.0 * (quad + jnp.sum(col_acc[...] * c_rows[...], axis=0, keepdims=True))
             quad_out[...] = jnp.broadcast_to(part, (SUB, lanes))
             for copy in quad_copies():
                 copy.start()
             quad_in[c] = quad_out[...]
 
         def direct(i, carry):
-            for u in range(UNROLL):
-                at = pl.multiple_of(i * (SUB * UNROLL) + u * SUB, SUB)
-                g_now = zero
-                for s in range(slots):
+            at = [pl.multiple_of((i * UNROLL + u) * SUB, SUB) for u in range(UNROLL)]
+            g_now = [zero] * UNROLL
+            for s in range(slots):
+                c_now = [
+                    jnp.broadcast_to(c_rows[n * slots + s : n * slots + s + 1, :], (SUB, lanes)) for n in range(chunks)
+                ]
+                for u in range(UNROLL):
                     for j in range(chunks):
-                        spot = pl.multiple_of(j * lanes + at, SUB)
+                        spot = pl.multiple_of(j * lanes + at[u], SUB)
                         dots = None
                         for n in range(chunks):
-                            part = tiles[s, pl.ds(spot, SUB), n * lanes : (n + 1) * lanes]
-                            here = n * slots + s
-                            term = part * c_rows[here : here + 1, :]
+                            term = tiles[s, pl.ds(spot, SUB), n * lanes : (n + 1) * lanes] * c_now[n]
                             dots = term if dots is None else dots + term
-                        g_now = jnp.where(
-                            lane_iota == j * slots + s, jnp.sum(dots, axis=1, keepdims=True), g_now
-                        )
-                g_cols[pl.ds(at, SUB), :] = g_now
+                        summed = jnp.sum(dots, axis=1, keepdims=True)
+                        g_now[u] = jnp.where(lane_iota == j * slots + s, summed, g_now[u])
+            for u in range(UNROLL):
+                g_cols[pl.ds(at[u], SUB), :] = g_now[u]
             return carry
 
         lax.fori_loop(0, lanes // (SUB * UNROLL), direct, 0)
@@ -448,7 +450,7 @@
                 copy.start()
             last_in[f] = last_out[...]
 
-        row_out[k] = select(put_row, g_cols[...].T)
+        row_out[k] = select(put_row, g_cols[...].T[: put_row.shape[1] // 2, :])
         for copy in row_returns(k):
             copy.start()
         row_back[k, c] = row_out[k, pl.ds(pl.multiple_of(c * slab, SUB), slab), :]
@@ -536,7 +538,7 @@
     blocks = frames // lanes
     slab = blocks * SUB
     reach_len = band_blocks.shape[0]
-    padded = -(-slots * chunks // lanes) * lanes
+    padded = -(-slots * chunks // (2 * SUB)) * 2 * SUB
     f32 = jnp.float32
     vmem = pl.BlockSpec(memory_space=pltpu.VMEM)
     dma = pltpu.SemaphoreType.DMA
@@ -568,14 +570,14 @@
         pltpu.VMEM((nc, SUB, lanes), f32),
         pltpu.VMEM((SUB, lanes), f32),
         pltpu.VMEM((nf, SUB, lanes), f32),
-        pltpu.VMEM((padded, 3 * nc * slab), bf16),
-        pltpu.VMEM((padded, 3 * nf * slab), bf16),
-        pltpu.VMEM((nc * slab, 3 * padded), bf16),
-        pltpu.VMEM((nf * slab, 3 * slots * chunks * SUB), bf16),
+        pltpu.VMEM((padded, 2 * nc * slab), bf16),
+        pltpu.VMEM((padded, 2 * nf * slab), bf16),
+        pltpu.VMEM((nc * slab, 2 * padded), bf16),
+        pltpu.VMEM((nf * slab, 2 * padded), bf16),
         pltpu.VMEM((lanes, padded), f32),
         pltpu.VMEM((padded, lanes), f32),
-        pltpu.VMEM((lanes, padded), f32),
-        pltpu.VMEM((slots * chunks * SUB, lanes), f32),
+        pltpu.VMEM((lanes, lanes), f32),
+        pltpu.VMEM((padded, lanes), f32),
         pltpu.VMEM((ITERS, SUB, lanes), f32),
         dma((slots,)),
         dma((7,)),

time: 49 us -> 48.6 us (level)
  no operation moved by 1% of the time
where the time goes in v6:
time: 48.6 us; the launch traced here: 48.4 us
  Pallas kernels  45.8 us (94%)
  local copies, waits for them, and re-layouts  1.32 us (3%)
  between operations  1.29 us (3%)
    pallas_call x1, Pallas kernels, per_device(): pl.pallas_call(functools.partial(kernel, nf, nc), out_shape=jax.ShapeDtyp...  45.8 us
    squeeze x1, local copies, waits for them, and re-layouts, per_device(): return (out[0], out[1])  1.32 us

profile of v6, /device:TPU:0, one launch (start us, length us, event | category | flops | bytes accessed | tf_op | source)
XLA Modules:
  0.0 48.4 jit_solution(5648155156343682346)
XLA Ops:
  1.3 45.8 %shard_map.95 = f32[2,6,256]{2,1,0:T(8,128)} custom-call(f32[6,256]{1,0:T(8,128)} %rhs_hbm.1, f32[6,6,256]{2,1,0:T(8,128)} %diag_hbm.1, f32[6,6,8,256]{3,2,1,0:T(8,128)} %bitcast.6, s32[1,256]{1,0:T(1,128)} %bitcast.7, f32[1,1,8,384,384]{4,3,2,1,0:T(8,128)} %tiles_hbm.1, s32[1,1,8]{2,1,0:T(1,128)} %rows_hbm.1, s32[1,1,8]{2,1,0:T(1,128)} %cols_hbm.1, ...), custom_call_target="tpu_custom_call" | custom-call | flops 18874368 | bytes 5013504 | tf_op jit(solution)/shard_map/pallas_call | solution.py:587
  47.0 1.3 %slice_bitcast_fusion = (f32[6,256]{1,0:T(8,128)}, f32[6,256]{1,0:T(8,128)}) fusion(f32[2,6,256]{2,1,0:T(8,128)} %shard_map.95), kind=kLoop, calls=%fused_computation | loop fusion | bytes 24576 | tf_op jit(solution)/shard_map/squeeze | solution.py:600

commit v7 on v6

--- a/solution.py
+++ b/solution.py
@@ -10,7 +10,7 @@
 ITERS = 4
 COMP = 6
 SUB = 8
-UNROLL = 4
+UNROLL = 8
 MESH = pl.DeviceIdType.MESH
 
 
@@ -322,10 +322,6 @@
     def step(k, carry):
         v = [vecs[k, h] for h in range(blocks)]
 
-        @pl.when(k > 0)
-        def _():
-            sent(k - 1)
-
         image = [zero] * blocks
         spill = zero
         for b in range(COMP):
@@ -385,6 +381,10 @@
         for copy in col_returns(k):
             copy.start()
         col_back[k, f] = col_out[k, pl.ds(pl.multiple_of(f * slab, SUB), slab), :]
+
+        @pl.when(k > 0)
+        def _():
+            sent(k - 1)
 
         unless(is_last, lambda: halo_copy(k).wait_recv())
         ext = v + [halo_in[k]]

time: 48.6 us -> 48 us (0.988)
  Pallas kernels: 45.8 us -> 45.2 us
    pallas_call x1, Pallas kernels: 45.8 us -> 45.2 us  [per_device(): pl.pallas_call(functools.partial(kernel, nf, nc), out_shape=jax.ShapeDtyp...]
where the time goes in v7:
time: 48 us; the launch traced here: 47.8 us
  Pallas kernels  45.2 us (94%)
  local copies, waits for them, and re-layouts  1.32 us (3%)
  between operations  1.29 us (3%)
    pallas_call x1, Pallas kernels, per_device(): pl.pallas_call(functools.partial(kernel, nf, nc), out_shape=jax.ShapeDtyp...  45.2 us
    squeeze x1, local copies, waits for them, and re-layouts, per_device(): return (out[0], out[1])  1.32 us

profile of v7, /device:TPU:0, one launch (start us, length us, event | category | flops | bytes accessed | tf_op | source)
XLA Modules:
  0.0 47.8 jit_solution(5399705362577109407)
XLA Ops:
  1.3 45.2 %shard_map.95 = f32[2,6,256]{2,1,0:T(8,128)} custom-call(f32[6,256]{1,0:T(8,128)} %rhs_hbm.1, f32[6,6,256]{2,1,0:T(8,128)} %diag_hbm.1, f32[6,6,8,256]{3,2,1,0:T(8,128)} %bitcast.6, s32[1,256]{1,0:T(1,128)} %bitcast.7, f32[1,1,8,384,384]{4,3,2,1,0:T(8,128)} %tiles_hbm.1, s32[1,1,8]{2,1,0:T(1,128)} %rows_hbm.1, s32[1,1,8]{2,1,0:T(1,128)} %cols_hbm.1, ...), custom_call_target="tpu_custom_call" | custom-call | flops 18874368 | bytes 5013504 | tf_op jit(solution)/shard_map/pallas_call | solution.py:587
  46.4 1.3 %slice_bitcast_fusion = (f32[6,256]{1,0:T(8,128)}, f32[6,256]{1,0:T(8,128)}) fusion(f32[2,6,256]{2,1,0:T(8,128)} %shard_map.95), kind=kLoop, calls=%fused_computation | loop fusion | bytes 24576 | tf_op jit(solution)/shard_map/squeeze | solution.py:600
